TPU v7x, 256 devices: a whole 4x4x8 slice. The times are simulated.
256 devices in a mesh: seq: 32 (over z, x), head: 8 (over y, core).
Axes of the slice: x: 4, y: 4, z: 8, core: 2. Of those that a mesh axis runs over, the one named last changes fastest.
Arguments:
- states: bfloat16 [16384, 4096], P('seq'), may hold values from -6 to 256
- w_query: bfloat16 [4096, 4096], P('seq', 'head'), may hold values from -1 to 1
- w_output: bfloat16 [4096, 4096], P('head', 'seq'), may hold values from -0.09375 to 0.09375
- kv_store: bfloat16 [256, 2, 128, 4096], P('seq', None, None, 'head'), may hold values from -140 to 140
- neighbour_ids: int32 [256, 2], P('seq'), may hold values from 0 to 255, as said below
- block_row: int32 [256], replicated, may hold values from 0 to 255, as said below
Outputs:
- mixed: bfloat16 [16384, 4096], P('seq', 'head')
Inputs may be any that keep to these rules, and one draw needn't show every extreme that they name: `block_row`: A permutation of 0 to 255; row r of kv_store lies on index r // 8 of seq. `neighbour_ids`: of the 16 neighbours of one index of seq, at most 2 lie in rows of kv_store held by any one index of seq; one such holder has exactly 2 of every index's neighbours.
All inputs are finite; a program needn't handle non-finite values.
Results may differ from a plain program's by a relative error of at most 0.019.
Values may be sent and summed in bfloat16 or wider, within the bound.
A program may use at most 128 MiB of HBM per device.

v0:
```python
import jax
import jax.numpy as jnp
from jax import lax
from jax.sharding import PartitionSpec as P

HD = 128
STRETCH = 64
NB_TOK = 128


def shifted(shard, axis, by):
    length = lax.axis_size(axis)
    pairs = [(i, i + by) for i in range(length) if 0 <= i + by < length]
    return lax.ppermute(shard, axis, pairs)


def partial_attend(query_block, kv_blocks):
    count, rows, width = query_block.shape
    nheads = width // HD
    qhead = query_block.reshape(count, rows, nheads, HD)
    keys = kv_blocks[:, 0].reshape(count, NB_TOK, nheads, HD)
    values = kv_blocks[:, 1].reshape(count, NB_TOK, nheads, HD)
    scores = jnp.einsum("nqhd,nkhd->nhqk", qhead, keys, preferred_element_type=jnp.float32) * (
        1.0 / HD**0.5
    )
    maxima = jnp.max(scores, axis=-1)
    weights = jnp.exp(scores - maxima[..., None]).astype(jnp.bfloat16)
    totals = jnp.sum(weights, axis=-1, dtype=jnp.float32)
    outputs = jnp.einsum("nhqk,nkhd->nqhd", weights, values, preferred_element_type=jnp.float32)
    return (outputs.reshape(count, rows, width), maxima, totals)


def combine_pair(outputs, maxima, totals):
    spans, neigh, rows, width = outputs.shape
    nheads = width // HD
    top = jnp.max(maxima, axis=1)
    factor = jnp.exp(maxima - top[:, None])
    denom = jnp.sum(factor * totals, axis=1)
    spread = jnp.transpose(factor, (0, 1, 3, 2))[..., None]
    numer = jnp.sum(outputs.reshape(spans, neigh, rows, nheads, HD) * spread, axis=1)
    result = numer / jnp.transpose(denom, (0, 2, 1))[..., None]
    return result.reshape(spans, rows, width).astype(jnp.bfloat16)


def local(states, w_query, w_output, kv_store, neighbour_ids, block_row):
    tok_rows = states.shape[0]
    width = w_query.shape[1]
    span_count, neigh = neighbour_ids.shape
    requests = span_count * neigh
    nseq = lax.axis_size("seq")
    slot_count = max(2, (2 * requests + nseq - 1) // nseq)
    blk_dev = kv_store.shape[0]
    position = lax.axis_index("seq")
    starts_here = position == 0
    next_starts = position == nseq - 1
    queries = jnp.dot(
        states,
        lax.all_gather(w_query, "seq", axis=0, tiled=True),
        preferred_element_type=jnp.float32,
    ).astype(jnp.bfloat16)
    leading = shifted(queries[: STRETCH - 1], "seq", -1)
    leading = jnp.where(next_starts, jnp.zeros_like(leading), leading)
    groups = jnp.concatenate([queries[STRETCH - 1 :], leading], axis=0).reshape(
        span_count, STRETCH, width
    )
    query_req = jnp.repeat(groups, neigh, axis=0)
    flat_ids = neighbour_ids.reshape(requests)
    table_cols = jnp.arange(block_row.shape[0], dtype=jnp.int32)
    store_row = jnp.sum(
        jnp.where(flat_ids[:, None] == table_cols[None, :], block_row[None, :], 0), axis=1
    )
    holders = store_row // blk_dev
    block_slot = store_row % blk_dev
    counter = jnp.arange(requests, dtype=jnp.int32)
    earlier = (holders[:, None] == holders[None, :]) & (counter[:, None] > counter[None, :])
    slot_rank = jnp.sum(earlier.astype(jnp.int32), axis=1)
    buffer_index = holders * slot_count + slot_rank
    slot_table = (
        jnp.zeros((nseq * slot_count,), jnp.int32)
        .at[buffer_index]
        .set(block_slot)
        .reshape(nseq, slot_count)
    )
    asked = lax.all_to_all(slot_table, "seq", split_axis=0, concat_axis=0, tiled=True)
    served = kv_store[asked.reshape(nseq * slot_count)].reshape(nseq, slot_count, 2, NB_TOK, width)
    fetched = lax.all_to_all(served, "seq", split_axis=0, concat_axis=0, tiled=True)
    kv_req = fetched.reshape(nseq * slot_count, 2, NB_TOK, width)[buffer_index]
    outputs, maxima, totals = partial_attend(query_req, kv_req)
    nheads = maxima.shape[1]
    context_groups = combine_pair(
        outputs.reshape(span_count, neigh, STRETCH, width),
        maxima.reshape(span_count, neigh, nheads, STRETCH),
        totals.reshape(span_count, neigh, nheads, STRETCH),
    )
    extended = context_groups.reshape(tok_rows, width)
    trailing = shifted(extended[tok_rows - STRETCH + 1 :], "seq", 1)
    trailing = jnp.where(starts_here, jnp.zeros_like(trailing), trailing)
    context = jnp.concatenate([trailing, extended[: tok_rows - STRETCH + 1]], axis=0)
    terms = jnp.dot(
        context,
        lax.all_gather(w_output, "seq", axis=1, tiled=True),
        preferred_element_type=jnp.float32,
    )
    return lax.psum_scatter(terms.astype(jnp.bfloat16), "head", scatter_dimension=1, tiled=True)


def solution(mesh):
    in_specs = (
        P("seq", None),
        P("seq", "head"),
        P("head", "seq"),
        P("seq", None, None, "head"),
        P("seq", None),
        P(),
    )
    out_specs = P("seq", "head")
    return jax.shard_map(local, mesh=mesh, in_specs=in_specs, out_specs=out_specs, check_vma=False)
```

profile of v0, /device:TPU:1, one launch (start us, length us, event | category | flops | bytes accessed | tf_op | source)
XLA Modules:
  0.0 574.7 jit_solution(16205739280007865709)
XLA Ops:
  6.5 0.0 copy-start
  6.5 0.9 copy.26
  7.4 0.1 eq.37
  7.5 0.9 select_reduce_fusion
  8.4 0.2 convert_reduce_fusion.1
  8.6 0.6 scatter_custom_fusion
  9.2 0.1 all_to_all.9
  9.3 20.2 %all_to_all.14 = s32[32,1,2]{2,1,0:T(1,128)S(1)} all-to-all(s32[32,1,2]{2,1,0:T(1,128)S(1)} %bitcast.62), channel_id=1, replica_groups=mesh['seq'=32,'head'=8] {'seq'}, dimensions={0} | all-to-all | bytes 512 | tf_op jit(solution)/shard_map/all_to_all | solution.py:84
  29.6 0.5 broadcast.198
  30.1 0.7 reduce.3
  30.8 0.1 reshape.152
  30.9 0.0 copy-done
  30.9 7.3 %gather_fusion = bf16[64,2,128,512]{3,2,1,0:T(8,128)(2,1)} fusion(bf16[8,2,128,512]{3,2,1,0:T(8,128)(2,1)S(1)} %copy-done, s32[1024]{0:T(1024)S(1)} %pad_clamp_fusion.1), kind=kCustom, calls=%fused_computation | custom fusion | bytes 33554688 | tf_op jit(solution)/shard_map/gather | solution.py:85
  38.3 5.2 all-to-all-start.1
  43.4 0.0 all-gather.3.cloned.1.call-start
  43.5 0.7 all-gather.3.cloned.1.call-update
  44.2 0.0 all-gather.5.cloned.1.call-start
  44.2 0.7 all-gather.5.cloned.1.call-update
  44.9 0.0 reduce-scatter.2.cloned.1.call-start
  45.0 173.1 %all-gather.3.cloned.1.call-done = bf16[4096,512]{1,0:T(8,128)(2,1)} async-done(((bf16[128,512]{1,0:T(8,128)(2,1)}), bf16[4096,512]{1,0:T(8,128)(2,1)}) %all-gather.3.cloned.1.call-update) | async-done | bytes 4194320 | tf_op jit(solution)/shard_map/all_gather | solution.py:58
  218.1 5.8 %convolution_convert_fusion.1 = bf16[512,512]{1,0:T(8,128)(2,1)S(1)} fusion(bf16[512,4096]{1,0:T(8,128)(2,1)} %param.6, bf16[4096,512]{1,0:T(8,128)(2,1)} %all-gather.3.cloned.1.call-done), kind=kOutput, calls=%fused_computation.8 | convolution fusion | flops 2147745792 | bytes 8912896 | tf_op jit(solution)/shard_map/dot_general | solution.py:56
  223.9 1.3 collective-permute-start
  225.2 0.1 slice.29
  225.3 17.3 %collective-permute-done = bf16[63,512]{1,0:T(8,128)(2,1)S(1)} collective-permute-done((bf16[63,512]{1,0:T(8,128)(2,1)S(1)}, bf16[63,512]{1,0:T(8,128)(2,1)S(1)}, u32[]{:S(2)}, u32[]{:S(2)}) %collective-permute-start) | collective-permute-done | bytes 64544 | tf_op jit(solution)/shard_map/ppermute | solution.py:14
  242.7 0.1 broadcast_in_dim.16
  242.8 0.3 reshape_reshape.3
  243.1 228.2 %all-to-all-done.1 = bf16[32,2,2,128,512]{4,3,2,1,0:T(8,128)(2,1)} async-done(((bf16[32,2,2,128,512]{4,3,2,1,0:T(8,128)(2,1)}), bf16[32,2,2,128,512]{4,3,2,1,0:T(8,128)(2,1)}, u32[]{:S(2)}, u32[]{:S(2)}) %all-to-all-start.1) | async-done | bytes 16777248 | tf_op jit(solution)/shard_map/all_to_all | solution.py:86
  471.2 8.6 %gather_fusion.1 = bf16[16,2,128,512]{3,2,1,0:T(8,128)(2,1)} fusion(bf16[64,2,128,512]{3,2,1,0:T(8,128)(2,1)} %bitcast.6, s32[1024]{0:T(1024)S(1)} %pad_clamp_fusion), kind=kCustom, calls=%fused_computation.1 | custom fusion | bytes 8388672 | tf_op jit(solution)/shard_map/gather | solution.py:87
  479.8 4.0 fusion.15
  483.8 3.9 copy.29
  487.7 2.4 copy.28
  490.1 2.4 multiply_reduce_fusion.1
  492.5 0.0 copy-start.2
  492.6 1.3 convert_reduce_fusion
  493.9 0.2 copy-done.2
  494.1 1.8 multiply_reduce_fusion
  495.9 0.3 divide_convert_fusion
  496.3 0.4 copy.33
  496.7 0.1 copy.42
  496.8 1.3 collective-permute-start.1
  498.1 1.3 collective-permute-done.1
  499.4 0.0 all-gather.5.cloned.1.call-done
  499.5 6.5 %convolution_convert_fusion = bf16[512,4096]{1,0:T(8,128)(2,1)} fusion(bf16[512,4096]{1,0:T(8,128)(2,1)} %all-gather.5.cloned.1.call-done, bf16[449,512]{1,0:T(8,128)(2,1)S(1)} %slice.33, bf16[63,512]{1,0:T(8,128)(2,1)S(1)} %broadcast_select_fusion.1), kind=kOutput, calls=%fused_computation.3 | convolution fusion | flops 2150629376 | bytes 8912896 | tf_op jit(solution)/shard_map/dot_general | solution.py:99
  505.9 0.0 copy-start.1
  505.9 0.0 reduce-scatter.2.cloned.1.call-update
  505.9 62.2 %reduce-scatter.2.cloned.1.call-done = bf16[512,512]{1,0:T(8,128)(2,1)} async-done(((bf16[512,4096]{1,0:T(8,128)(2,1)}), bf16[512,512]{1,0:T(8,128)(2,1)}) %reduce-scatter.2.cloned.1.call-update) | async-done | bytes 524304 | tf_op jit(solution)/shard_map/reduce_scatter | solution.py:104
  568.2 0.0 copy-done.1
  (13 shorter events, 0.2 us)
Async XLA Ops:
  6.5 24.4 %copy-start = (bf16[8,2,128,512]{3,2,1,0:T(8,128)(2,1)S(1)}, bf16[8,2,128,512]{3,2,1,0:T(8,128)(2,1)}, u32[]{:S(2)}) copy-start(bf16[8,2,128,512]{3,2,1,0:T(8,128)(2,1)} %param.9) | copy-start | bytes 6291460
  38.3 433.0 %all-to-all-start.1 = ((bf16[32,2,2,128,512]{4,3,2,1,0:T(8,128)(2,1)}), bf16[32,2,2,128,512]{4,3,2,1,0:T(8,128)(2,1)}, u32[]{:S(2)}, u32[]{:S(2)}) async-start(bf16[32,2,2,128,512]{4,3,2,1,0:T(8,128)(2,1)} %bitcast.54), calls=%async_computation.1 | async-start | bytes 33554432 | tf_op jit(solution)/shard_map/all_to_all | solution.py:86
  43.4 174.6 %all-gather.3.cloned.1.call-start = ((), (), s32[]{:S(2)}) async-start(), calls=%async_computation.3 | async-start | bytes 4325376 | tf_op jit(solution)/shard_map/all_gather | solution.py:58
  44.2 455.3 %all-gather.5.cloned.1.call-start = ((), (), s32[]{:S(2)}) async-start(), calls=%async_computation.4 | async-start | bytes 4325376 | tf_op jit(solution)/shard_map/all_gather | solution.py:101
  44.9 523.2 %reduce-scatter.2.cloned.1.call-start = ((), (), s32[]{:S(2)}) async-start(), calls=%async_computation.5 | async-start | bytes 4718592 | tf_op jit(solution)/shard_map/reduce_scatter | solution.py:104
  223.9 18.7 %collective-permute-start = (bf16[63,512]{1,0:T(8,128)(2,1)S(1)}, bf16[63,512]{1,0:T(8,128)(2,1)S(1)}, u32[]{:S(2)}, u32[]{:S(2)}) collective-permute-start(bf16[63,512]{1,0:T(8,128)(2,1)S(1)} %slice.30), channel_id=1, source_target_pairs={{8,0},{16,8},{24,16},{32,24},{40,32},{48,40},{56,48},{64,56},{72,6... | collective-permute-start | bytes 193544 | tf_op jit(solution)/shard_map/ppermute | solution.py:14
  492.5 1.6 copy-start.2
  496.8 2.6 collective-permute-start.1
  505.9 62.2 %copy-start.1 = (bf16[8,2,128,512]{3,2,1,0:T(8,128)(2,1)S(1)}, bf16[8,2,128,512]{3,2,1,0:T(8,128)(2,1)}, u32[]{:S(2)}) copy-start(bf16[8,2,128,512]{3,2,1,0:T(8,128)(2,1)} %param.9) | copy-start | bytes 6291460
Sparse Core Ops, SparseCore 0:
  46.8 171.1 all-gather.2
  220.5 262.8 all-gather.4
  506.1 62.0 reduce-scatter.1
where the time goes:
time: 577 us; the launch traced here: 575 us
  waiting for transfers between devices  483 us (84%)
  local copies, waits for them, and re-layouts  29.8 us (5%)
  blocking collectives  20.2 us (4%)
  matrix products  16.4 us (3%)
  between operations  13.4 us (2%)
  starting transfers between devices  7.86 us (1%)
    all_to_all x1, waiting for transfers between devices, local(): lax.all_to_all(served, 'seq', split_axis=0, concat_axis=0, tiled=True)  228 us
    all_gather x1, waiting for transfers between devices, local(): lax.all_gather(w_query, 'seq', axis=0, tiled=True)  173 us
    reduce_scatter x1, waiting for transfers between devices, local(): lax.psum_scatter(terms.astype(jnp.bfloat16), 'head', scatter_dimension=1,...  62.2 us
    all_to_all x1, blocking collectives, local(): lax.all_to_all(slot_table, 'seq', split_axis=0, concat_axis=0, tiled=True)  20.2 us
    ppermute x2, waiting for transfers between devices, shifted(): return lax.ppermute(shard, axis, pairs)  18.6 us
  transfers between devices with their start and end apart: 6, of which 5 were waited for; matrix products, arithmetic and copies ran while one was open for 6% of the time, Pallas kernels for 0%

commit v1 on v0

v1 whole, which is shorter than its diff:
```python
import jax
import jax.numpy as jnp
from jax import lax
from jax.experimental import pallas as pl
from jax.experimental.pallas import tpu as pltpu
from jax.sharding import PartitionSpec as P

HD = 128
STRETCH = 64
NB_TOK = 128
NX, NZ, NY = 4, 8, 4
NSEQ, NHEAD = NX * NZ, 2 * NY
T = 512
W = 512
QT = 128
NEG = -1e30
SCALE = 1.0 / HD**0.5
MESH = pl.DeviceIdType.MESH
N_COPIES = 192
BF = jnp.bfloat16
F32 = jnp.float32


def quarter(i):
    return pl.ds(i * QT, QT)


def part(i):
    return pl.ds(pl.multiple_of(i * QT, QT), QT)


def kernel(
    states, wq, wo, kv, rows, out,
    st, wqg, acc, qall, kvr, oatt, ml, ro, sw, rw, wog, rall, rsm,
    ctx, ps, pr, tf, t2s, t2r, t1s, t1r, ost, lsem, osem, ssem, rsem,
):
    s, h = lax.axis_index("seq"), lax.axis_index("head")
    z, x, y, c = s // NX, s % NX, h // 2, h % 2
    up, down = (s + NX) % NSEQ, (s + NSEQ - NX) % NSEQ
    right, left = z * NX + (x + 1) % NX, z * NX + (x + NX - 1) % NX
    after, before = (s + 1) % NSEQ, (s + NSEQ - 1) % NSEQ
    yup, ydown, twin = (h + 2) % NHEAD, (h + NHEAD - 2) % NHEAD, h + 1 - 2 * c
    count = [0]
    started = {}

    def send(src, dst, seq=None, head=None):
        n = count[0]
        count[0] += 1
        copy = pltpu.make_async_remote_copy(
            src_ref=src,
            dst_ref=dst,
            send_sem=ssem.at[n],
            recv_sem=rsem.at[n],
            device_id=(s if seq is None else seq, h if head is None else head),
            device_id_type=MESH,
        )
        copy.start()
        started[id(copy)] = copy
        return copy

    barrier = pltpu.get_barrier_semaphore()
    peers = [((s + NX * i) % NSEQ, h) for i in range(1, NZ)]
    peers += [(right, h), (left, h), (after, h), (before, h)]
    peers += [(s, (h + i) % NHEAD) for i in range(1, NHEAD)]
    for peer in peers:
        pl.semaphore_signal(barrier, inc=1, device_id=peer, device_id_type=MESH)

    own = [
        pltpu.make_async_copy(states, st.at[pl.ds(0, T)], lsem.at[0]),
        pltpu.make_async_copy(wq, wqg.at[0, part(x)], lsem.at[1]),
        pltpu.make_async_copy(wo, wog.at[z, x], lsem.at[2]),
        pltpu.make_async_copy(kv, kvr.at[pl.ds(x * 8, 8)], lsem.at[3]),
        pltpu.make_async_copy(rows, rall.at[0], lsem.at[4]),
    ]
    for copy in own:
        copy.start()
    pl.semaphore_wait(barrier, len(peers))

    wx = {}
    wx[1] = send(wq, wqg.at[0, part(x)], seq=right)
    wx[3] = send(wq, wqg.at[0, part(x)], seq=left)
    wup, wdown = {}, {}

    def wsend(j, d, first=False):
        at = part((x + NX - d) % NX)
        src = wq if first else wqg.at[j, at]
        if j < 3 or (j == 3 and d in (0, 1)):
            wup[j + 1, d] = send(src, wqg.at[j + 1, at], seq=up)
        if j in (0, 7, 6) or (j == 5 and d in (2, 3)):
            wdown[(j + 7) % 8, d] = send(src, wqg.at[(j + 7) % 8, at], seq=down)

    wsend(0, 0, first=True)
    oup, odown = {}, {}

    def osend(step):
        if step == 1:
            oup[1] = send(wo, wog.at[z, x], seq=up)
            odown[1] = send(wo, wog.at[z, x], seq=down)
            return
        oup[step - 1].wait_recv()
        a = (z + NZ - step + 1) % NZ
        if step < 4:
            oup[step] = send(wog.at[a, x], wog.at[a, x], seq=up)
        else:
            half = pl.ds(0, 256)
            oup[step] = send(wog.at[a, x, half], wog.at[a, x, half], seq=up)
        odown[step - 1].wait_recv()
        b = (z + step - 1) % NZ
        if step < 4:
            odown[step] = send(wog.at[b, x], wog.at[b, x], seq=down)
        else:
            half = pl.ds(256, 256)
            odown[step] = send(wog.at[b, x, half], wog.at[b, x, half], seq=down)

    osend(1)
    rids = [
        send(rows, rall.at[i], seq=(s + NX * i) % NSEQ) for i in range(1, NZ)
    ]
    hcols = pl.ds(pl.multiple_of(h * W, W), W)
    tail = st.at[pl.ds(T, 64), hcols]
    first_rows = send(states.at[pl.ds(0, 64), hcols], tail, seq=before)

    own[1].wait()
    wx[1].wait_recv()
    lo, hi = (x + 3) % NX, (x + 1) % NX
    halves = [
        wqg.at[0, pl.ds(pl.multiple_of(lo * QT, QT), 64)],
        wqg.at[0, pl.ds(pl.multiple_of(hi * QT + 64, 64), 64)],
    ]
    wx[2] = send(halves[0], halves[0], seq=right)
    wsend(0, 1)
    wx[3].wait_recv()
    wx[4] = send(halves[1], halves[1], seq=left)
    wsend(0, 3)

    def blocks(xo, half):
        return kvr.at[pl.ds(xo * 8 + 4 * half, 4)]

    kvs = {}
    kvs["r0"] = send(kv.at[pl.ds(0, 4)], blocks(x, 0), seq=right)
    kvs["l1"] = send(kv.at[pl.ds(4, 4)], blocks(x, 1), seq=left)
    kvs["r1"] = send(kv.at[pl.ds(4, 4)], blocks(x, 1), seq=right)
    kvs["l0"] = send(kv.at[pl.ds(0, 4)], blocks(x, 0), seq=left)

    wx[2].wait_recv()
    wx[4].wait_recv()
    wsend(0, 2)

    first_rows.wait_recv()
    others = [send(tail, tail, head=(h + i) % NHEAD) for i in range(1, NHEAD)]
    osend(2)

    def multiply(j):
        cols = pl.ds(pl.multiple_of(((z + NZ - j) % NZ) * 512, 512), 512)

        def body(i, _):
            r = pl.ds(pl.multiple_of(i * 192, 64), 192)
            term = jnp.dot(st[r, cols], wqg[j], preferred_element_type=F32)
            acc[r, :] = term if j == 0 else acc[r, :] + term
            return 0

        lax.fori_loop(0, 3, body, 0)

    order = (0, 1, 3, 2)
    for j in (1, 2, 3):
        for d in order:
            wup[j, d].wait_recv()
            wdown[8 - j, d].wait_recv()
            wsend(j, d)
            wsend(8 - j, d)
        if j == 1:
            own[0].wait()
            for copy in others:
                copy.wait_recv()
            for copy in others:
                copy.wait_send()
                del started[id(copy)]

            @pl.when(s == NSEQ - 1)
            def _():
                st[pl.ds(T, 64), :] = jnp.zeros((64, NHEAD * W), BF)

            multiply(0)
        if j == 3:
            kvs["r0"].wait_recv()
            kvs["r2"] = send(blocks(lo, 0), blocks(lo, 0), seq=right)
            kvs["l1"].wait_recv()
            kvs["l2"] = send(blocks(hi, 1), blocks(hi, 1), seq=left)
        if j < 3:
            osend(j + 2)
        multiply(j)
        multiply(8 - j)
    for d in (0, 1):
        wup[4, d].wait_recv()
    for d in (2, 3):
        wdown[4, d].wait_recv()
    multiply(4)

    qup, qdown = {}, {}

    def qsend(j, q):
        at = qall.at[j, quarter(q)]
        if j < 3 or (j == 3 and q < 2):
            qup[j + 1, q] = send(at, qall.at[j + 1, quarter(q)], seq=up)
        if j in (0, 7, 6) or (j == 5 and q >= 2):
            k = (j + 7) % 8
            qdown[k, q] = send(at, qall.at[k, quarter(q)], seq=down)

    for q in range(4):
        qall[0, quarter(q), :] = acc[pl.ds(63 + q * QT, QT), :].astype(BF)
        qsend(0, q)

    for copy in rids:
        copy.wait_recv()
    own[4].wait()
    scalars = pltpu.make_async_copy(rall, rsm, lsem.at[5])
    scalars.start()
    oup[4].wait_recv()
    odown[4].wait_recv()
    scalars.wait()

    for j in (1, 2):
        for q in range(4):
            qup[j, q].wait_recv()
            qdown[8 - j, q].wait_recv()
            qsend(j, q)
            qsend(8 - j, q)

    own[3].wait()
    for name in ("r1", "l0", "r2", "l2"):
        kvs[name].wait_recv()

    own[2].wait()
    oxs = {}
    oxs["r"] = send(wog.at[:, x], wog.at[:, x], seq=right)
    oxs["l"] = send(wog.at[:, x], wog.at[:, x], seq=left)

    lane = lax.broadcasted_iota(jnp.int32, (STRETCH, 128), 1)
    wide = lax.broadcasted_iota(jnp.int32, (1, 2 * NB_TOK), 1)

    def attend(j, g):
        r0, r1 = rsm[j, g, 0], rsm[j, g, 1]
        off0 = jnp.where(r0 // 32 == z, 0.0, NEG)
        off1 = jnp.where(r1 // 32 == z, 0.0, NEG)
        bias = jnp.where(wide < NB_TOK, off0, off1)
        b0, b1 = r0 % 32, r1 % 32
        at = pl.ds(pl.multiple_of(g * STRETCH, STRETCH), STRETCH)
        stats = jnp.zeros((STRETCH, 128), F32)
        for i in range(W // HD):
            cols = slice(i * HD, i * HD + HD)
            keys = jnp.concatenate([kvr[b0, 0, :, cols], kvr[b1, 0, :, cols]], axis=0)
            scores = lax.dot_general(
                qall[j, at, cols], keys, (((1,), (1,)), ((), ())), preferred_element_type=F32
            )
            scores = scores * SCALE + bias
            top = jnp.max(scores, axis=1, keepdims=True)
            weights = jnp.exp(scores - top).astype(BF)
            total = jnp.sum(weights.astype(F32), axis=1, keepdims=True)
            values = jnp.concatenate([kvr[b0, 1, :, cols], kvr[b1, 1, :, cols]], axis=0)
            got = jnp.dot(weights, values, preferred_element_type=F32)
            oatt[j, at, cols] = got.astype(BF)
            stats = jnp.where(lane == i, top, jnp.where(lane == i + 4, total, stats))
        ml[j, at, :] = stats

    def attend_slots(a, b):
        def body(i, _):
            attend(jnp.where(i < 8, a, b), i % 8)
            return 0

        lax.fori_loop(0, 8 if a == b else 16, body, 0)

    attend_slots(1, 7)
    for q in range(4):
        if q < 2:
            qup[3, q].wait_recv()
            qsend(3, q)
        else:
            qdown[5, q].wait_recv()
            qsend(5, q)
    attend_slots(2, 6)
    for q in range(4):
        if q < 2:
            qdown[5, q].wait_recv()
        else:
            qup[3, q].wait_recv()
    attend_slots(3, 5)
    for q in range(4):
        (qup if q < 2 else qdown)[4, q].wait_recv()
    attend_slots(4, 4)

    sent, sent_stats = {}, {}

    def rsend(way, k, q, rows_at):
        j = k if way == 0 else 8 - k
        there = down if way == 0 else up
        sent[way, k, q] = send(oatt.at[j, rows_at], ro.at[way, k - 1, rows_at], seq=there)
        sent_stats[way, k, q] = send(sw.at[j, q], rw.at[way, k - 1, q], seq=there)

    def turn_out(j, q):
        sw[j, q] = jnp.transpose(ml[j, quarter(q), :])[0:8, :]

    def turn_in(way, k, q):
        wire = jnp.concatenate([rw[way, k - 1, q], jnp.zeros((120, 128), F32)], axis=0)
        return jnp.transpose(wire)

    def merge(way, k, q, start, size):
        j = k if way == 0 else 8 - k
        at = pl.ds(q * QT + start, size)
        a = turn_in(way, k + 1, q)[start : start + size]
        b = ml[j, at, :]
        top = jnp.maximum(a, b)
        ea, eb = jnp.exp(a - top), jnp.exp(b - top)
        total = a * pltpu.roll(ea, 4, axis=1) + b * pltpu.roll(eb, 4, axis=1)
        lanes = lax.broadcasted_iota(jnp.int32, (size, 128), 1)
        ml[j, at, :] = jnp.where(lanes < 4, top, jnp.where(lanes < 8, total, 0.0))
        for i in range(W // HD):
            cols = slice(i * HD, i * HD + HD)
            mixed = ea[:, i : i + 1] * ro[way, k, at, cols].astype(F32)
            mixed = mixed + eb[:, i : i + 1] * oatt[j, at, cols].astype(F32)
            oatt[j, at, cols] = mixed.astype(BF)

    for q in range(4):
        turn_out(4, q)
        rsend(0, 4, q, pl.ds(q * QT, 64))
        rsend(1, 4, q, pl.ds(q * QT + 64, 64))
    for k in (3, 2, 1):
        if k == 2:
            attend_slots(0, 0)
            oxs["r"].wait_recv()
            lower = wog.at[pl.ds(0, 4), lo]
            oxs["r2"] = send(lower, lower, seq=right)
            oxs["l"].wait_recv()
            upper = wog.at[pl.ds(4, 4), hi]
            oxs["l2"] = send(upper, upper, seq=left)
        for q in range(4):
            for way in (0, 1):
                sent[way, k + 1, q].wait_recv()
                sent_stats[way, k + 1, q].wait_recv()
                if k == 3:
                    merge(way, k, q, 64 * way, 64)
                else:
                    merge(way, k, q, 0, QT)
                turn_out(k if way == 0 else 8 - k, q)
                rsend(way, k, q, quarter(q))
    for name in ("r2", "l2"):
        oxs[name].wait_recv()

    def weights_for(g):
        return jnp.concatenate([wog[g, i] for i in range(NX)], axis=1)

    def join(q):
        at = quarter(q)
        for way in (0, 1):
            sent[way, 1, q].wait_recv()
            sent_stats[way, 1, q].wait_recv()
        a, b, e = turn_in(0, 1, q), turn_in(1, 1, q), ml[0, at, :]
        top = jnp.maximum(jnp.maximum(a, b), e)
        fa, fb, fe = jnp.exp(a - top), jnp.exp(b - top), jnp.exp(e - top)
        total = a * pltpu.roll(fa, 4, axis=1) + b * pltpu.roll(fb, 4, axis=1)
        total = total + e * pltpu.roll(fe, 4, axis=1)
        total = pltpu.roll(total, 124, axis=1)
        fa, fb, fe = fa / total, fb / total, fe / total
        for i in range(W // HD):
            cols = slice(i * HD, i * HD + HD)
            mixed = fa[:, i : i + 1] * ro[0, 0, at, cols].astype(F32)
            mixed = mixed + fb[:, i : i + 1] * ro[1, 0, at, cols].astype(F32)
            mixed = mixed + fe[:, i : i + 1] * oatt[0, at, cols].astype(F32)
            ctx[q, :, cols] = mixed.astype(BF)

    pairs, seconds, thirds, written = {}, {}, {}, []

    def for_twin(q):
        def body(i, _):
            g = 2 * ((y + i) % NY) + 1 - c
            ps[q, i] = jnp.dot(ctx[q], weights_for(g), preferred_element_type=F32).astype(BF)
            return 0

        lax.fori_loop(0, NY, body, 0)
        pairs[q] = send(ps.at[q], pr.at[q], head=twin)

    def for_self(q):
        pairs[q].wait_recv()

        def body(i, _):
            g = 2 * ((y + i) % NY) + c
            term = jnp.dot(ctx[q], weights_for(g), preferred_element_type=F32)
            tf[q, i] = term + pr[q, i].astype(F32)
            return 0

        lax.fori_loop(0, NY, body, 0)
        t2s[q] = tf[q, 2].astype(BF)
        a, b = pl.ds(0, 64), pl.ds(64, 64)
        seconds[q] = (
            send(t2s.at[q, a], t2r.at[q, a], head=yup),
            send(t2s.at[q, b], t2r.at[q, b], head=ydown),
        )

    def pass_on(q):
        for copy in seconds[q]:
            copy.wait_recv()
        t1s[q, 0, 0:64] = (tf[q, 1, 0:64] + t2r[q, 0:64].astype(F32)).astype(BF)
        t1s[q, 0, 64:128] = tf[q, 1, 64:128].astype(BF)
        t1s[q, 1, 0:64] = tf[q, 3, 0:64].astype(BF)
        t1s[q, 1, 64:128] = (tf[q, 3, 64:128] + t2r[q, 64:128].astype(F32)).astype(BF)
        thirds[q] = (
            send(t1s.at[q, 0], t1r.at[q, 0], head=yup),
            send(t1s.at[q, 1], t1r.at[q, 1], head=ydown),
        )

    def finish(q):
        for copy in thirds[q]:
            copy.wait_recv()
        total = tf[q, 0] + t1r[q, 0].astype(F32) + t1r[q, 1].astype(F32)
        ost[q] = total.astype(BF)
        copy = pltpu.make_async_copy(ost.at[q], out.at[quarter(q)], osem.at[q])
        copy.start()
        written.append(copy)

    for step in range(7):
        for q in range(4):
            if step == q:
                join(q)
                for_twin(q)
        for lag, act in ((1, for_self), (2, pass_on), (3, finish)):
            if 0 <= step - lag < 4:
                act(step - lag)
    for copy in written:
        copy.wait()
    for copy in started.values():
        copy.wait_send()


def exchange(states, w_query, w_output, kv_store, rows):
    anywhere = pl.BlockSpec(memory_space=pl.ANY)
    vm = pltpu.VMEM
    return pl.pallas_call(
        kernel,
        out_shape=jax.ShapeDtypeStruct((T, W), BF),
        in_specs=[anywhere] * 4 + [pl.BlockSpec(memory_space=vm)],
        out_specs=anywhere,
        scratch_shapes=[
            vm((T + 64, NHEAD * W), BF),
            vm((NZ, 512, W), BF),
            vm((T + 64, W), F32),
            vm((NZ, T, W), BF),
            vm((32, 2, NB_TOK, W), BF),
            vm((NZ, T, W), BF),
            vm((NZ, T, 128), F32),
            vm((2, 4, T, W), BF),
            vm((NZ, 4, 8, 128), F32),
            vm((2, 4, 4, 8, 128), F32),
            vm((NZ, NX, W, 128), BF),
            vm((NZ, 8, 128), jnp.int32),
            pltpu.SMEM((NZ, 8, 128), jnp.int32),
            vm((4, QT, W), BF),
            vm((4, NY, QT, 512), BF),
            vm((4, NY, QT, 512), BF),
            vm((4, NY, QT, 512), F32),
            vm((4, QT, 512), BF),
            vm((4, QT, 512), BF),
            vm((4, 2, QT, 512), BF),
            vm((4, 2, QT, 512), BF),
            vm((4, QT, 512), BF),
            pltpu.SemaphoreType.DMA((6,)),
            pltpu.SemaphoreType.DMA((4,)),
            pltpu.SemaphoreType.DMA((N_COPIES,)),
            pltpu.SemaphoreType.DMA((N_COPIES,)),
        ],
        compiler_params=pltpu.CompilerParams(
            collective_id=0, has_side_effects=True, vmem_limit_bytes=60 * 2**20
        ),
        cost_estimate=pl.CostEstimate(
            flops=8 * 10**9, bytes_accessed=8 * 2**20, transcendentals=2**22
        ),
    )(states, w_query, w_output, kv_store, rows)


def local(states, w_query, w_output, kv_store, neighbour_ids, block_row):
    ids = neighbour_ids[:, :, None]
    cols = jnp.arange(block_row.shape[0], dtype=jnp.int32)
    rows = jnp.sum(jnp.where(ids == cols, block_row, 0), axis=2)
    rows = jnp.pad(rows, ((0, 0), (0, 126)))
    mixed = exchange(states, w_query, w_output, kv_store, rows)
    keep = T - STRETCH + 1
    trailing = lax.ppermute(mixed[keep:], "seq", [(i, i + 1) for i in range(NSEQ - 1)])
    return jnp.concatenate([trailing, mixed[:keep]], axis=0)


def solution(mesh):
    in_specs = (
        P("seq", None),
        P("seq", "head"),
        P("head", "seq"),
        P("seq", None, None, "head"),
        P("seq", None),
        P(),
    )
    out_specs = P("seq", "head")
    return jax.shard_map(local, mesh=mesh, in_specs=in_specs, out_specs=out_specs, check_vma=False)
```

time: 577 us -> 226 us (0.39)
  waiting for transfers between devices: 483 us -> 0.25 us
  Pallas kernels: 0 us -> 216 us
  local copies, waits for them, and re-layouts: 29.8 us -> 2.6 us
  blocking collectives: 20.2 us -> 0 us
  matrix products: 16.4 us -> 0 us
  between operations: 13.4 us -> 0.03 us
  starting transfers between devices: 7.86 us -> 1.55 us
    all_to_all x1 -> x0, waiting for transfers between devices: 228 us -> none  [local(): lax.all_to_all(served, 'seq', split_axis=0, concat_axis=0, tiled=True)]
    pallas_call x0 -> x1, Pallas kernels: none -> 216 us  [exchange(): pl.pallas_call(kernel, out_shape=jax.ShapeDtypeStruct((T, W), BF), in_spe...]
    all_gather x2 -> x0, waiting for transfers between devices: 173 us -> none  [the longest x1 173 us: local(): lax.all_gather(w_query, 'seq', axis=0, tiled=True)]
    reduce_scatter x1 -> x0, waiting for transfers between devices: 62.2 us -> none  [local(): lax.psum_scatter(terms.astype(jnp.bfloat16), 'head', scatter_dimension=1,...]
    all_to_all x1 -> x0, blocking collectives: 20.2 us -> none  [local(): lax.all_to_all(slot_table, 'seq', split_axis=0, concat_axis=0, tiled=True)]
    ppermute x2 -> x1, waiting for transfers between devices: 18.6 us -> 0.25 us  [local(): lax.ppermute(mixed[keep:], 'seq', [(i, i + 1) for i in range(NSEQ - 1)])]
    dot_general x4 -> x0, matrix products: 16.4 us -> none  [the longest x1 6.46 us: local(): jnp.dot(context, lax.all_gather(w_output, 'seq', axis=1, tiled=True), pre...]
    gather x2 -> x0, local copies, waits for them, and re-layouts: 15.9 us -> none  [the longest x1 8.55 us: local(): kv_req = fetched.reshape(nseq * slot_count, 2, NB_TOK, width)[buffer_index]]
  transfers between devices with their start and end apart: 6 -> 1, of which waited for: 5 -> 1; matrix products, arithmetic and copies ran while one was open for 6% -> 0% of each run, Pallas kernels for 0% -> 0%
where the time goes in v1:
time: 226 us; the launch traced here: 223 us
  Pallas kernels  216 us (96%)
  local copies, waits for them, and re-layouts  2.6 us (1%)
    pallas_call x1, Pallas kernels, exchange(): pl.pallas_call(kernel, out_shape=jax.ShapeDtypeStruct((T, W), BF), in_spe...  216 us
  transfers between devices with their start and end apart: 1, of which 1 were waited for; matrix products, arithmetic and copies ran while one was open for 0% of the time, Pallas kernels for 0%

profile of v1, /device:TPU:1, one launch (start us, length us, event | category | flops | bytes accessed | tf_op | source)
XLA Modules:
  0.0 222.6 jit_solution(3741444146515612719)
XLA Ops:
  0.0 0.9 select_reduce_fusion
  0.9 0.1 copy.8
  1.0 0.6 pad.4.rows
  1.6 216.3 %shard_map.64 = bf16[512,512]{1,0:T(8,128)(2,1)} custom-call(bf16[512,4096]{1,0:T(8,128)(2,1)} %states.1, bf16[128,512]{1,0:T(8,128)(2,1)} %wq.1, bf16[512,128]{1,0:T(8,128)(2,1)} %wo.1, bf16[8,2,128,512]{3,2,1,0:T(8,128)(2,1)} %kv.1, s32[8,128]{1,0:T(8,128)} %pad.4.rows), custom_call_target="tpu_custom_call" | custom-call | flops 8000000000 | bytes 8388608 | tf_op jit(solution)/shard_map/pallas_call | solution.py:436
  218.0 0.9 slice.6
  218.8 1.6 collective-permute-start
  220.4 1.1 slice.7
  221.4 0.3 collective-permute-done
  221.7 0.9 pad_maximum_fusion
Async XLA Ops:
  218.8 2.9 %collective-permute-start = (bf16[63,512]{1,0:T(8,128)(2,1)S(1)}, bf16[63,512]{1,0:T(8,128)(2,1)S(1)}, u32[]{:S(2)}, u32[]{:S(2)}) collective-permute-start(bf16[63,512]{1,0:T(8,128)(2,1)S(1)} %slice.6), channel_id=1, source_target_pairs={{0,8},{8,16},{16,24},{24,32},{32,40},{40,48},{48,56},{56,64},{64,7... | collective-permute-start | bytes 193544 | tf_op jit(solution)/shard_map/ppermute | solution.py:485

commit v2 on v1

--- a/solution.py
+++ b/solution.py
@@ -30,9 +30,9 @@
 
 
 def kernel(
-    states, wq, wo, kv, rows, out,
-    st, wqg, acc, qall, kvr, oatt, ml, ro, sw, rw, wog, rall, rsm,
-    ctx, ps, pr, tf, t2s, t2r, t1s, t1r, ost, lsem, osem, ssem, rsem,
+    states, wq, wo, kv, ids, table, out,
+    st, wqg, acc, qall, kvr, oatt, ml, ro, sw, rw, wog, iall, ism,
+    ctx, ps, pr, tf, t2s, t2r, t1s, t1r, kraw, fin, edge_s, edge_r, ost, lsem, osem, ssem, rsem,
 ):
     s, h = lax.axis_index("seq"), lax.axis_index("head")
     z, x, y, c = s // NX, s % NX, h // 2, h % 2
@@ -69,11 +69,22 @@
         pltpu.make_async_copy(states, st.at[pl.ds(0, T)], lsem.at[0]),
         pltpu.make_async_copy(wq, wqg.at[0, part(x)], lsem.at[1]),
         pltpu.make_async_copy(wo, wog.at[z, x], lsem.at[2]),
-        pltpu.make_async_copy(kv, kvr.at[pl.ds(x * 8, 8)], lsem.at[3]),
-        pltpu.make_async_copy(rows, rall.at[0], lsem.at[4]),
+        pltpu.make_async_copy(kv.at[:, 1], kvr.at[pl.ds(x * 8, 8), 1], lsem.at[3]),
+        pltpu.make_async_copy(ids, iall.at[0], lsem.at[4]),
+        pltpu.make_async_copy(kv.at[:, 0], kraw, lsem.at[6]),
     ]
-    for copy in own:
-        copy.start()
+    for i in (5, 3, 1, 0, 2, 4):
+        own[i].start()
+
+    own[5].wait()
+
+    def turn_keys(b, _):
+        for i in range(W // HD):
+            cols = slice(i * HD, i * HD + HD)
+            kvr[x * 8 + b, 0, :, cols] = jnp.transpose(kraw[b, :, cols])
+        return 0
+
+    lax.fori_loop(0, 8, turn_keys, 0)
     pl.semaphore_wait(barrier, len(peers))
 
     wx = {}
@@ -114,7 +125,7 @@
 
     osend(1)
     rids = [
-        send(rows, rall.at[i], seq=(s + NX * i) % NSEQ) for i in range(1, NZ)
+        send(ids, iall.at[i], seq=(s + NX * i) % NSEQ) for i in range(1, NZ)
     ]
     hcols = pl.ds(pl.multiple_of(h * W, W), W)
     tail = st.at[pl.ds(T, 64), hcols]
@@ -133,14 +144,16 @@
     wx[4] = send(halves[1], halves[1], seq=left)
     wsend(0, 3)
 
+    own[3].wait()
+
     def blocks(xo, half):
         return kvr.at[pl.ds(xo * 8 + 4 * half, 4)]
 
     kvs = {}
-    kvs["r0"] = send(kv.at[pl.ds(0, 4)], blocks(x, 0), seq=right)
-    kvs["l1"] = send(kv.at[pl.ds(4, 4)], blocks(x, 1), seq=left)
-    kvs["r1"] = send(kv.at[pl.ds(4, 4)], blocks(x, 1), seq=right)
-    kvs["l0"] = send(kv.at[pl.ds(0, 4)], blocks(x, 0), seq=left)
+    kvs["r0"] = send(blocks(x, 0), blocks(x, 0), seq=right)
+    kvs["l1"] = send(blocks(x, 1), blocks(x, 1), seq=left)
+    kvs["r1"] = send(blocks(x, 1), blocks(x, 1), seq=right)
+    kvs["l0"] = send(blocks(x, 0), blocks(x, 0), seq=left)
 
     wx[2].wait_recv()
     wx[4].wait_recv()
@@ -213,7 +226,7 @@
     for copy in rids:
         copy.wait_recv()
     own[4].wait()
-    scalars = pltpu.make_async_copy(rall, rsm, lsem.at[5])
+    scalars = pltpu.make_async_copy(iall, ism, lsem.at[5])
     scalars.start()
     oup[4].wait_recv()
     odown[4].wait_recv()
@@ -226,7 +239,6 @@
             qsend(j, q)
             qsend(8 - j, q)
 
-    own[3].wait()
     for name in ("r1", "l0", "r2", "l2"):
         kvs[name].wait_recv()
 
@@ -239,7 +251,7 @@
     wide = lax.broadcasted_iota(jnp.int32, (1, 2 * NB_TOK), 1)
 
     def attend(j, g):
-        r0, r1 = rsm[j, g, 0], rsm[j, g, 1]
+        r0, r1 = table[ism[j, 0, g]], table[ism[j, 1, g]]
         off0 = jnp.where(r0 // 32 == z, 0.0, NEG)
         off1 = jnp.where(r1 // 32 == z, 0.0, NEG)
         bias = jnp.where(wide < NB_TOK, off0, off1)
@@ -248,10 +260,8 @@
         stats = jnp.zeros((STRETCH, 128), F32)
         for i in range(W // HD):
             cols = slice(i * HD, i * HD + HD)
-            keys = jnp.concatenate([kvr[b0, 0, :, cols], kvr[b1, 0, :, cols]], axis=0)
-            scores = lax.dot_general(
-                qall[j, at, cols], keys, (((1,), (1,)), ((), ())), preferred_element_type=F32
-            )
+            keys = jnp.concatenate([kvr[b0, 0, :, cols], kvr[b1, 0, :, cols]], axis=1)
+            scores = jnp.dot(qall[j, at, cols], keys, preferred_element_type=F32)
             scores = scores * SCALE + bias
             top = jnp.max(scores, axis=1, keepdims=True)
             weights = jnp.exp(scores - top).astype(BF)
@@ -264,10 +274,11 @@
 
     def attend_slots(a, b):
         def body(i, _):
-            attend(jnp.where(i < 8, a, b), i % 8)
+            for g in range(4):
+                attend(jnp.where(i < 2, a, b), (i % 2) * 4 + g)
             return 0
 
-        lax.fori_loop(0, 8 if a == b else 16, body, 0)
+        lax.fori_loop(0, 2 if a == b else 4, body, 0)
 
     attend_slots(1, 7)
     for q in range(4):
@@ -319,32 +330,6 @@
             mixed = mixed + eb[:, i : i + 1] * oatt[j, at, cols].astype(F32)
             oatt[j, at, cols] = mixed.astype(BF)
 
-    for q in range(4):
-        turn_out(4, q)
-        rsend(0, 4, q, pl.ds(q * QT, 64))
-        rsend(1, 4, q, pl.ds(q * QT + 64, 64))
-    for k in (3, 2, 1):
-        if k == 2:
-            attend_slots(0, 0)
-            oxs["r"].wait_recv()
-            lower = wog.at[pl.ds(0, 4), lo]
-            oxs["r2"] = send(lower, lower, seq=right)
-            oxs["l"].wait_recv()
-            upper = wog.at[pl.ds(4, 4), hi]
-            oxs["l2"] = send(upper, upper, seq=left)
-        for q in range(4):
-            for way in (0, 1):
-                sent[way, k + 1, q].wait_recv()
-                sent_stats[way, k + 1, q].wait_recv()
-                if k == 3:
-                    merge(way, k, q, 64 * way, 64)
-                else:
-                    merge(way, k, q, 0, QT)
-                turn_out(k if way == 0 else 8 - k, q)
-                rsend(way, k, q, quarter(q))
-    for name in ("r2", "l2"):
-        oxs[name].wait_recv()
-
     def weights_for(g):
         return jnp.concatenate([wog[g, i] for i in range(NX)], axis=1)
 
@@ -411,32 +396,102 @@
         for copy in thirds[q]:
             copy.wait_recv()
         total = tf[q, 0] + t1r[q, 0].astype(F32) + t1r[q, 1].astype(F32)
-        ost[q] = total.astype(BF)
-        copy = pltpu.make_async_copy(ost.at[q], out.at[quarter(q)], osem.at[q])
+        fin[pl.ds(64 + q * QT, QT), :] = total
+
+    def give_edge():
+        edge_s[...] = fin[pl.ds(T, 64), :].astype(BF)
+        return send(edge_s, edge_r, seq=after)
+
+    def take_edge(copy):
+        copy.wait_recv()
+        fin[pl.ds(0, 64), :] = jnp.where(s == 0, 0.0, edge_r[...].astype(F32))
+
+    def write(i):
+        ost[i] = fin[pl.ds(i * QT + 1, QT), :].astype(BF)
+        copy = pltpu.make_async_copy(ost.at[i], out.at[quarter(i)], osem.at[i])
         copy.start()
         written.append(copy)
 
-    for step in range(7):
-        for q in range(4):
-            if step == q:
-                join(q)
-                for_twin(q)
-        for lag, act in ((1, for_self), (2, pass_on), (3, finish)):
-            if 0 <= step - lag < 4:
-                act(step - lag)
+    def open_wave(q):
+        turn_out(4, q)
+        rsend(0, 4, q, pl.ds(q * QT, 64))
+        rsend(1, 4, q, pl.ds(q * QT + 64, 64))
+
+    def hop(k, q):
+        for way in (0, 1):
+            sent[way, k + 1, q].wait_recv()
+            sent_stats[way, k + 1, q].wait_recv()
+            if k == 3:
+                merge(way, k, q, 64 * way, 64)
+            else:
+                merge(way, k, q, 0, QT)
+            turn_out(k if way == 0 else 8 - k, q)
+            rsend(way, k, q, quarter(q))
+
+    for q in (3, 0):
+        open_wave(q)
+    for q in (3, 0):
+        hop(3, q)
+    attend_slots(0, 0)
+    for q in (3, 0):
+        hop(2, q)
+    oxs["r"].wait_recv()
+    lower = wog.at[pl.ds(0, 4), lo]
+    oxs["r2"] = send(lower, lower, seq=right)
+    oxs["l"].wait_recv()
+    upper = wog.at[pl.ds(4, 4), hi]
+    oxs["l2"] = send(upper, upper, seq=left)
+    for q in (3, 0):
+        hop(1, q)
+    for q in (1, 2):
+        open_wave(q)
+    for q in (3, 0):
+        join(q)
+    for q in (1, 2):
+        hop(3, q)
+    for name in ("r2", "l2"):
+        oxs[name].wait_recv()
+    for q in (3, 0):
+        for_twin(q)
+    for q in (3, 0):
+        for_self(q)
+    for q in (1, 2):
+        hop(2, q)
+    for q in (3, 0):
+        pass_on(q)
+    for q in (1, 2):
+        hop(1, q)
+    finish(3)
+    edge = give_edge()
+    finish(0)
+    take_edge(edge)
+    write(0)
+    join(1)
+    for_twin(1)
+    join(2)
+    for_twin(2)
+    for_self(1)
+    for_self(2)
+    pass_on(1)
+    pass_on(2)
+    finish(1)
+    write(1)
+    finish(2)
+    write(2)
+    write(3)
     for copy in written:
         copy.wait()
     for copy in started.values():
         copy.wait_send()
 
 
-def exchange(states, w_query, w_output, kv_store, rows):
+def exchange(states, w_query, w_output, kv_store, ids, table):
     anywhere = pl.BlockSpec(memory_space=pl.ANY)
     vm = pltpu.VMEM
     return pl.pallas_call(
         kernel,
         out_shape=jax.ShapeDtypeStruct((T, W), BF),
-        in_specs=[anywhere] * 4 + [pl.BlockSpec(memory_space=vm)],
+        in_specs=[anywhere] * 5 + [pl.BlockSpec(memory_space=pltpu.SMEM)],
         out_specs=anywhere,
         scratch_shapes=[
             vm((T + 64, NHEAD * W), BF),
@@ -450,8 +505,8 @@
             vm((NZ, 4, 8, 128), F32),
             vm((2, 4, 4, 8, 128), F32),
             vm((NZ, NX, W, 128), BF),
-            vm((NZ, 8, 128), jnp.int32),
-            pltpu.SMEM((NZ, 8, 128), jnp.int32),
+            vm((NZ, 2, 8), jnp.int32),
+            pltpu.SMEM((NZ, 2, 8), jnp.int32),
             vm((4, QT, W), BF),
             vm((4, NY, QT, 512), BF),
             vm((4, NY, QT, 512), BF),
@@ -460,8 +515,12 @@
             vm((4, QT, 512), BF),
             vm((4, 2, QT, 512), BF),
             vm((4, 2, QT, 512), BF),
+            vm((8, NB_TOK, W), BF),
+            vm((T + 64, W), F32),
+            vm((64, W), BF),
+            vm((64, W), BF),
             vm((4, QT, 512), BF),
-            pltpu.SemaphoreType.DMA((6,)),
+            pltpu.SemaphoreType.DMA((8,)),
             pltpu.SemaphoreType.DMA((4,)),
             pltpu.SemaphoreType.DMA((N_COPIES,)),
             pltpu.SemaphoreType.DMA((N_COPIES,)),
@@ -472,18 +531,11 @@
         cost_estimate=pl.CostEstimate(
             flops=8 * 10**9, bytes_accessed=8 * 2**20, transcendentals=2**22
         ),
-    )(states, w_query, w_output, kv_store, rows)
+    )(states, w_query, w_output, kv_store, ids, table)
 
 
 def local(states, w_query, w_output, kv_store, neighbour_ids, block_row):
-    ids = neighbour_ids[:, :, None]
-    cols = jnp.arange(block_row.shape[0], dtype=jnp.int32)
-    rows = jnp.sum(jnp.where(ids == cols, block_row, 0), axis=2)
-    rows = jnp.pad(rows, ((0, 0), (0, 126)))
-    mixed = exchange(states, w_query, w_output, kv_store, rows)
-    keep = T - STRETCH + 1
-    trailing = lax.ppermute(mixed[keep:], "seq", [(i, i + 1) for i in range(NSEQ - 1)])
-    return jnp.concatenate([trailing, mixed[:keep]], axis=0)
+    return exchange(states, w_query, w_output, kv_store, neighbour_ids.T, block_row)
 
 
 def solution(mesh):

time: 226 us -> 178 us (0.79); the launches traced: 223 us -> 178 us
  Pallas kernels: 216 us -> 176 us
    pallas_call x1, Pallas kernels: 216 us -> 176 us  [exchange(): pl.pallas_call(kernel, out_shape=jax.ShapeDtypeStruct((T, W), BF), in_spe...]
  transfers between devices with their start and end apart: 1 -> 0, of which waited for: 1 -> 0; matrix products, arithmetic and copies ran while one was open for 0% -> 0% of each run, Pallas kernels for 0% -> 0%
where the time goes in v2:
time: 178 us
  Pallas kernels  176 us (99%)
  local copies, waits for them, and re-layouts  1.87 us (1%)
    pallas_call x1, Pallas kernels, exchange(): pl.pallas_call(kernel, out_shape=jax.ShapeDtypeStruct((T, W), BF), in_spe...  176 us

profile of v2, /device:TPU:1, one launch (start us, length us, event | category | flops | bytes accessed | tf_op | source)
XLA Modules:
  0.0 178.2 jit_solution(17180077798747600262)
XLA Ops:
  0.0 176.3 %shard_map.64 = bf16[512,512]{1,0:T(8,128)(2,1)} custom-call(bf16[512,4096]{1,0:T(8,128)(2,1)} %states.1, bf16[128,512]{1,0:T(8,128)(2,1)} %wq.1, bf16[512,128]{1,0:T(8,128)(2,1)} %wo.1, bf16[8,2,128,512]{3,2,1,0:T(8,128)(2,1)} %kv.1, s32[2,8]{1,0:T(2,128)} %bitcast.1, s32[256]{0:T(256)} %table.1), custom_call_target="tpu_custom_call" | custom-call | flops 8000000000 | bytes 8388608 | tf_op jit(solution)/shard_map/pallas_call | solution.py:491
  176.3 1.9 %copy.8 = bf16[512,512]{1,0:T(8,128)(2,1)} copy(bf16[512,512]{1,0:T(8,128)(2,1)} %shard_map.64) | data formatting | bytes 1048576

commit v3 on v2

--- a/solution.py
+++ b/solution.py
@@ -16,7 +16,8 @@
 NEG = -1e30
 SCALE = 1.0 / HD**0.5
 MESH = pl.DeviceIdType.MESH
-N_COPIES = 192
+N_COPIES = 232
+PA, PB = 80, 48
 BF = jnp.bfloat16
 F32 = jnp.float32
 
@@ -76,6 +77,43 @@
     for i in (5, 3, 1, 0, 2, 4):
         own[i].start()
 
+    pl.semaphore_wait(barrier, len(peers))
+
+    def arows(d, start=0, size=PA):
+        return pl.ds(pl.multiple_of(((x + NX - d) % NX) * QT + start, 16), size)
+
+    def brows(xo, start=0, size=PB):
+        return pl.ds(pl.multiple_of(xo * QT + PA + start, 16), size)
+
+    wx, bup, bdown = {}, {}, {}
+    wup, wdown = {}, {}
+
+    def bsend(step):
+        src = wq.at[pl.ds(PA, PB)]
+        if step == 1:
+            bup[1] = send(src, wqg.at[1, brows(x)], seq=up)
+            bdown[1] = send(src, wqg.at[7, brows(x)], seq=down)
+            return
+        at = brows(x) if step < 4 else brows(x, 0, 32)
+        bup[step - 1].wait_recv()
+        bup[step] = send(wqg.at[step - 1, at], wqg.at[step, at], seq=up)
+        at = brows(x) if step < 4 else brows(x, 32, 16)
+        bdown[step - 1].wait_recv()
+        bdown[step] = send(wqg.at[9 - step, at], wqg.at[8 - step, at], seq=down)
+
+    def wsend(j, d, first=False):
+        at = arows(d)
+        src = wq.at[pl.ds(0, PA)] if first else wqg.at[j, at]
+        if j < 3 or (j == 3 and d in (0, 1)):
+            wup[j + 1, d] = send(src, wqg.at[j + 1, at], seq=up)
+        if j in (0, 7, 6) or (j == 5 and d in (2, 3)):
+            wdown[(j + 7) % 8, d] = send(src, wqg.at[(j + 7) % 8, at], seq=down)
+
+    wx[1] = send(wq.at[pl.ds(0, PA)], wqg.at[0, arows(0)], seq=right)
+    wx[3] = send(wq.at[pl.ds(0, PA)], wqg.at[0, arows(0)], seq=left)
+    bsend(1)
+    wsend(0, 0, first=True)
+
     own[5].wait()
 
     def turn_keys(b, _):
@@ -85,22 +123,50 @@
         return 0
 
     lax.fori_loop(0, 8, turn_keys, 0)
-    pl.semaphore_wait(barrier, len(peers))
-
-    wx = {}
-    wx[1] = send(wq, wqg.at[0, part(x)], seq=right)
-    wx[3] = send(wq, wqg.at[0, part(x)], seq=left)
-    wup, wdown = {}, {}
-
-    def wsend(j, d, first=False):
-        at = part((x + NX - d) % NX)
-        src = wq if first else wqg.at[j, at]
-        if j < 3 or (j == 3 and d in (0, 1)):
-            wup[j + 1, d] = send(src, wqg.at[j + 1, at], seq=up)
-        if j in (0, 7, 6) or (j == 5 and d in (2, 3)):
-            wdown[(j + 7) % 8, d] = send(src, wqg.at[(j + 7) % 8, at], seq=down)
-
-    wsend(0, 0, first=True)
+    wx[1].wait_recv()
+    wx[2] = send(wqg.at[0, arows(1, 0, 48)], wqg.at[0, arows(1, 0, 48)], seq=right)
+    wx[3].wait_recv()
+    wx[4] = send(wqg.at[0, arows(3, 48, 32)], wqg.at[0, arows(3, 48, 32)], seq=left)
+    bsend(2)
+    wsend(0, 1)
+    wsend(0, 3)
+    iids = [send(ids, iall.at[i], seq=(s + NX * i) % NSEQ) for i in range(1, NZ)]
+    hcols = pl.ds(pl.multiple_of(h * W, W), W)
+    tail = st.at[pl.ds(T, 64), hcols]
+    first_rows = send(states.at[pl.ds(0, 64), hcols], tail, seq=before)
+    bsend(3)
+
+    lo, hi = (x + 3) % NX, (x + 1) % NX
+    kvright, kvleft = {}, {}
+    own[3].wait()
+
+    def kvsend(n):
+        a, b = n % 8, (n + 4) % 8
+        if n < 8:
+            xa, xb = x, x
+        else:
+            xa, xb = lo, hi
+            kvright[n - 8].wait_recv()
+            kvleft[n - 8].wait_recv()
+        kvright[n] = send(kvr.at[xa * 8 + a], kvr.at[xa * 8 + a], seq=right)
+        kvleft[n] = send(kvr.at[xb * 8 + b], kvr.at[xb * 8 + b], seq=left)
+
+    kvsend(0)
+    wx[2].wait_recv()
+    wx[4].wait_recv()
+    wsend(0, 2)
+    bsend(4)
+    kvsend(1)
+    first_rows.wait_recv()
+    others = [send(tail, tail, head=(h + i) % NHEAD) for i in range(1, NHEAD)]
+    own[1].wait()
+    bup[4].wait_recv()
+    bdown[4].wait_recv()
+    bx = {}
+    bx["r"] = send(wqg.at[:, brows(x)], wqg.at[:, brows(x)], seq=right)
+    bx["l"] = send(wqg.at[:, brows(x)], wqg.at[:, brows(x)], seq=left)
+    kvsend(2)
+
     oup, odown = {}, {}
 
     def osend(step):
@@ -123,46 +189,6 @@
             half = pl.ds(256, 256)
             odown[step] = send(wog.at[b, x, half], wog.at[b, x, half], seq=down)
 
-    osend(1)
-    rids = [
-        send(ids, iall.at[i], seq=(s + NX * i) % NSEQ) for i in range(1, NZ)
-    ]
-    hcols = pl.ds(pl.multiple_of(h * W, W), W)
-    tail = st.at[pl.ds(T, 64), hcols]
-    first_rows = send(states.at[pl.ds(0, 64), hcols], tail, seq=before)
-
-    own[1].wait()
-    wx[1].wait_recv()
-    lo, hi = (x + 3) % NX, (x + 1) % NX
-    halves = [
-        wqg.at[0, pl.ds(pl.multiple_of(lo * QT, QT), 64)],
-        wqg.at[0, pl.ds(pl.multiple_of(hi * QT + 64, 64), 64)],
-    ]
-    wx[2] = send(halves[0], halves[0], seq=right)
-    wsend(0, 1)
-    wx[3].wait_recv()
-    wx[4] = send(halves[1], halves[1], seq=left)
-    wsend(0, 3)
-
-    own[3].wait()
-
-    def blocks(xo, half):
-        return kvr.at[pl.ds(xo * 8 + 4 * half, 4)]
-
-    kvs = {}
-    kvs["r0"] = send(blocks(x, 0), blocks(x, 0), seq=right)
-    kvs["l1"] = send(blocks(x, 1), blocks(x, 1), seq=left)
-    kvs["r1"] = send(blocks(x, 1), blocks(x, 1), seq=right)
-    kvs["l0"] = send(blocks(x, 0), blocks(x, 0), seq=left)
-
-    wx[2].wait_recv()
-    wx[4].wait_recv()
-    wsend(0, 2)
-
-    first_rows.wait_recv()
-    others = [send(tail, tail, head=(h + i) % NHEAD) for i in range(1, NHEAD)]
-    osend(2)
-
     def multiply(j):
         cols = pl.ds(pl.multiple_of(((z + NZ - j) % NZ) * 512, 512), 512)
 
@@ -182,6 +208,18 @@
             wsend(j, d)
             wsend(8 - j, d)
         if j == 1:
+            osend(1)
+            bx["r"].wait_recv()
+            at = (pl.ds(0, 4), brows(lo))
+            bx["r2"] = send(wqg.at[at], wqg.at[at], seq=right)
+            bx["l"].wait_recv()
+            at = (pl.ds(4, 4), brows(hi))
+            bx["l2"] = send(wqg.at[at], wqg.at[at], seq=left)
+            kvsend(3)
+        if j == 2:
+            osend(2)
+            kvsend(4)
+            kvsend(5)
             own[0].wait()
             for copy in others:
                 copy.wait_recv()
@@ -193,16 +231,14 @@
             def _():
                 st[pl.ds(T, 64), :] = jnp.zeros((64, NHEAD * W), BF)
 
-            multiply(0)
         if j == 3:
-            kvs["r0"].wait_recv()
-            kvs["r2"] = send(blocks(lo, 0), blocks(lo, 0), seq=right)
-            kvs["l1"].wait_recv()
-            kvs["l2"] = send(blocks(hi, 1), blocks(hi, 1), seq=left)
-        if j < 3:
-            osend(j + 2)
-        multiply(j)
-        multiply(8 - j)
+            osend(3)
+            kvsend(6)
+            kvsend(7)
+            bx["r2"].wait_recv()
+            bx["l2"].wait_recv()
+            for n in (0, 1, 7, 2, 6, 3, 5):
+                multiply(n)
     for d in (0, 1):
         wup[4, d].wait_recv()
     for d in (2, 3):
@@ -223,13 +259,13 @@
         qall[0, quarter(q), :] = acc[pl.ds(63 + q * QT, QT), :].astype(BF)
         qsend(0, q)
 
-    for copy in rids:
+    kvsend(8)
+    kvsend(9)
+    for copy in iids:
         copy.wait_recv()
     own[4].wait()
     scalars = pltpu.make_async_copy(iall, ism, lsem.at[5])
     scalars.start()
-    oup[4].wait_recv()
-    odown[4].wait_recv()
     scalars.wait()
 
     for j in (1, 2):
@@ -238,9 +274,16 @@
             qdown[8 - j, q].wait_recv()
             qsend(j, q)
             qsend(8 - j, q)
-
-    for name in ("r1", "l0", "r2", "l2"):
-        kvs[name].wait_recv()
+        if j == 1:
+            osend(4)
+            kvsend(10)
+            kvsend(11)
+
+    for n in range(4, 12):
+        kvright[n].wait_recv()
+        kvleft[n].wait_recv()
+    oup[4].wait_recv()
+    odown[4].wait_recv()
 
     own[2].wait()
     oxs = {}
@@ -354,31 +397,29 @@
 
     pairs, seconds, thirds, written = {}, {}, {}, []
 
+    far_first = (2, 1, 3, 0)
+
     def for_twin(q):
-        def body(i, _):
+        for i in far_first:
             g = 2 * ((y + i) % NY) + 1 - c
             ps[q, i] = jnp.dot(ctx[q], weights_for(g), preferred_element_type=F32).astype(BF)
-            return 0
-
-        lax.fori_loop(0, NY, body, 0)
-        pairs[q] = send(ps.at[q], pr.at[q], head=twin)
+            pairs[q, i] = send(ps.at[q, i], pr.at[q, i], head=twin)
 
     def for_self(q):
-        pairs[q].wait_recv()
-
-        def body(i, _):
+        for i in far_first:
             g = 2 * ((y + i) % NY) + c
             term = jnp.dot(ctx[q], weights_for(g), preferred_element_type=F32)
-            tf[q, i] = term + pr[q, i].astype(F32)
-            return 0
-
-        lax.fori_loop(0, NY, body, 0)
-        t2s[q] = tf[q, 2].astype(BF)
-        a, b = pl.ds(0, 64), pl.ds(64, 64)
-        seconds[q] = (
-            send(t2s.at[q, a], t2r.at[q, a], head=yup),
-            send(t2s.at[q, b], t2r.at[q, b], head=ydown),
-        )
+            pairs[q, i].wait_recv()
+            term = term + pr[q, i].astype(F32)
+            if i != 2:
+                tf[q, i] = term
+                continue
+            t2s[q] = term.astype(BF)
+            a, b = pl.ds(0, 64), pl.ds(64, 64)
+            seconds[q] = (
+                send(t2s.at[q, a], t2r.at[q, a], head=yup),
+                send(t2s.at[q, b], t2r.at[q, b], head=ydown),
+            )
 
     def pass_on(q):
         for copy in seconds[q]:
@@ -464,14 +505,14 @@
     finish(3)
     edge = give_edge()
     finish(0)
-    take_edge(edge)
-    write(0)
     join(1)
     for_twin(1)
     join(2)
     for_twin(2)
     for_self(1)
     for_self(2)
+    take_edge(edge)
+    write(0)
     pass_on(1)
     pass_on(2)
     finish(1)

time: 178 us -> 178 us (level); the launches traced: 178 us -> 176 us
  Pallas kernels: 176 us -> 174 us
    pallas_call x1, Pallas kernels: 176 us -> 174 us  [exchange(): pl.pallas_call(kernel, out_shape=jax.ShapeDtypeStruct((T, W), BF), in_spe...]
where the time goes in v3:
time: 178 us; the launch traced here: 176 us
  Pallas kernels  174 us (98%)
  local copies, waits for them, and re-layouts  1.87 us (1%)
    pallas_call x1, Pallas kernels, exchange(): pl.pallas_call(kernel, out_shape=jax.ShapeDtypeStruct((T, W), BF), in_spe...  174 us

profile of v3, /device:TPU:1, one launch (start us, length us, event | category | flops | bytes accessed | tf_op | source)
XLA Modules:
  0.0 176.3 jit_solution(6271411438034227739)
XLA Ops:
  0.0 174.4 %shard_map.64 = bf16[512,512]{1,0:T(8,128)(2,1)} custom-call(bf16[512,4096]{1,0:T(8,128)(2,1)} %states.1, bf16[128,512]{1,0:T(8,128)(2,1)} %wq.1, bf16[512,128]{1,0:T(8,128)(2,1)} %wo.1, bf16[8,2,128,512]{3,2,1,0:T(8,128)(2,1)} %kv.1, s32[2,8]{1,0:T(2,128)} %bitcast.1, s32[256]{0:T(256)} %table.1), custom_call_target="tpu_custom_call" | custom-call | flops 8000000000 | bytes 8388608 | tf_op jit(solution)/shard_map/pallas_call | solution.py:532
  174.5 1.9 %copy.8 = bf16[512,512]{1,0:T(8,128)(2,1)} copy(bf16[512,512]{1,0:T(8,128)(2,1)} %shard_map.64) | data formatting | bytes 1048576

commit v4 on v3

--- a/solution.py
+++ b/solution.py
@@ -17,7 +17,8 @@
 SCALE = 1.0 / HD**0.5
 MESH = pl.DeviceIdType.MESH
 N_COPIES = 232
-PA, PB = 80, 48
+PA, PB = 96, 32
+AU, BU = (PA // 16 + 1) // 2 * 16, (PB // 16 + 1) // 2 * 16
 BF = jnp.bfloat16
 F32 = jnp.float32
 
@@ -32,7 +33,7 @@
 
 def kernel(
     states, wq, wo, kv, ids, table, out,
-    st, wqg, acc, qall, kvr, oatt, ml, ro, sw, rw, wog, iall, ism,
+    st, wqg, acc, qall, kv0, kv1, kv2, kv3, oatt, ml, ro, sw, rw, wog, iall, ism,
     ctx, ps, pr, tf, t2s, t2r, t1s, t1r, kraw, fin, edge_s, edge_r, ost, lsem, osem, ssem, rsem,
 ):
     s, h = lax.axis_index("seq"), lax.axis_index("head")
@@ -41,6 +42,7 @@
     right, left = z * NX + (x + 1) % NX, z * NX + (x + NX - 1) % NX
     after, before = (s + 1) % NSEQ, (s + NSEQ - 1) % NSEQ
     yup, ydown, twin = (h + 2) % NHEAD, (h + NHEAD - 2) % NHEAD, h + 1 - 2 * c
+    kvh = (kv0, kv1, kv2, kv3)
     count = [0]
     started = {}
 
@@ -70,11 +72,19 @@
         pltpu.make_async_copy(states, st.at[pl.ds(0, T)], lsem.at[0]),
         pltpu.make_async_copy(wq, wqg.at[0, part(x)], lsem.at[1]),
         pltpu.make_async_copy(wo, wog.at[z, x], lsem.at[2]),
-        pltpu.make_async_copy(kv.at[:, 1], kvr.at[pl.ds(x * 8, 8), 1], lsem.at[3]),
-        pltpu.make_async_copy(ids, iall.at[0], lsem.at[4]),
-        pltpu.make_async_copy(kv.at[:, 0], kraw, lsem.at[6]),
+        pltpu.make_async_copy(ids, iall.at[0], lsem.at[3]),
+        pltpu.make_async_copy(kv.at[:, 0], kraw, lsem.at[4]),
     ]
-    for i in (5, 3, 1, 0, 2, 4):
+    own_values = [
+        pltpu.make_async_copy(
+            kv.at[:, 1, :, pl.ds(i * HD, HD)], kvh[i].at[pl.ds(x * 8, 8), 1], lsem.at[8 + i]
+        )
+        for i in range(4)
+    ]
+    own[4].start()
+    for copy in own_values:
+        copy.start()
+    for i in (1, 0, 2, 3):
         own[i].start()
 
     pl.semaphore_wait(barrier, len(peers))
@@ -94,10 +104,10 @@
             bup[1] = send(src, wqg.at[1, brows(x)], seq=up)
             bdown[1] = send(src, wqg.at[7, brows(x)], seq=down)
             return
-        at = brows(x) if step < 4 else brows(x, 0, 32)
+        at = brows(x) if step < 4 else brows(x, 0, BU)
         bup[step - 1].wait_recv()
         bup[step] = send(wqg.at[step - 1, at], wqg.at[step, at], seq=up)
-        at = brows(x) if step < 4 else brows(x, 32, 16)
+        at = brows(x) if step < 4 else brows(x, BU, PB - BU)
         bdown[step - 1].wait_recv()
         bdown[step] = send(wqg.at[9 - step, at], wqg.at[8 - step, at], seq=down)
 
@@ -114,19 +124,19 @@
     bsend(1)
     wsend(0, 0, first=True)
 
-    own[5].wait()
+    own[4].wait()
 
     def turn_keys(b, _):
         for i in range(W // HD):
             cols = slice(i * HD, i * HD + HD)
-            kvr[x * 8 + b, 0, :, cols] = jnp.transpose(kraw[b, :, cols])
+            kvh[i][x * 8 + b, 0] = jnp.transpose(kraw[b, :, cols])
         return 0
 
     lax.fori_loop(0, 8, turn_keys, 0)
     wx[1].wait_recv()
-    wx[2] = send(wqg.at[0, arows(1, 0, 48)], wqg.at[0, arows(1, 0, 48)], seq=right)
+    wx[2] = send(wqg.at[0, arows(1, 0, AU)], wqg.at[0, arows(1, 0, AU)], seq=right)
     wx[3].wait_recv()
-    wx[4] = send(wqg.at[0, arows(3, 48, 32)], wqg.at[0, arows(3, 48, 32)], seq=left)
+    wx[4] = send(wqg.at[0, arows(3, AU, PA - AU)], wqg.at[0, arows(3, AU, PA - AU)], seq=left)
     bsend(2)
     wsend(0, 1)
     wsend(0, 3)
@@ -138,18 +148,27 @@
 
     lo, hi = (x + 3) % NX, (x + 1) % NX
     kvright, kvleft = {}, {}
-    own[3].wait()
+    for copy in own_values:
+        copy.wait()
+
+    def blocks(i, xo, half):
+        return kvh[i].at[pl.ds(xo * 8 + 4 * half, 4)]
 
     def kvsend(n):
-        a, b = n % 8, (n + 4) % 8
-        if n < 8:
-            xa, xb = x, x
+        i, turn = n // 3, n % 3
+        if turn < 2:
+            a, b = blocks(i, x, turn), blocks(i, x, 1 - turn)
         else:
-            xa, xb = lo, hi
-            kvright[n - 8].wait_recv()
-            kvleft[n - 8].wait_recv()
-        kvright[n] = send(kvr.at[xa * 8 + a], kvr.at[xa * 8 + a], seq=right)
-        kvleft[n] = send(kvr.at[xb * 8 + b], kvr.at[xb * 8 + b], seq=left)
+            a, b = blocks(i, lo, 0), blocks(i, hi, 1)
+            kvright[3 * i].wait_recv()
+            kvleft[3 * i].wait_recv()
+        kvright[n] = send(a, a, seq=right)
+        kvleft[n] = send(b, b, seq=left)
+
+    def kvwait(i):
+        for n in (3 * i + 1, 3 * i + 2):
+            kvright[n].wait_recv()
+            kvleft[n].wait_recv()
 
     kvsend(0)
     wx[2].wait_recv()
@@ -219,7 +238,7 @@
         if j == 2:
             osend(2)
             kvsend(4)
-            kvsend(5)
+            kvsend(6)
             own[0].wait()
             for copy in others:
                 copy.wait_recv()
@@ -233,7 +252,7 @@
 
         if j == 3:
             osend(3)
-            kvsend(6)
+            kvsend(5)
             kvsend(7)
             bx["r2"].wait_recv()
             bx["l2"].wait_recv()
@@ -259,88 +278,94 @@
         qall[0, quarter(q), :] = acc[pl.ds(63 + q * QT, QT), :].astype(BF)
         qsend(0, q)
 
-    kvsend(8)
     kvsend(9)
     for copy in iids:
         copy.wait_recv()
-    own[4].wait()
+    own[3].wait()
     scalars = pltpu.make_async_copy(iall, ism, lsem.at[5])
     scalars.start()
     scalars.wait()
 
-    for j in (1, 2):
+    lane = lax.broadcasted_iota(jnp.int32, (STRETCH, 128), 1)
+    wide = lax.broadcasted_iota(jnp.int32, (1, 2 * NB_TOK), 1)
+
+    def attend(j, g, i):
+        r0, r1 = table[ism[j, 0, g]], table[ism[j, 1, g]]
+        off0 = jnp.where(r0 // 32 == z, 0.0, NEG)
+        off1 = jnp.where(r1 // 32 == z, 0.0, NEG)
+        bias = jnp.where(wide < NB_TOK, off0, off1)
+        b0, b1 = r0 % 32, r1 % 32
+        at = pl.ds(g * STRETCH, STRETCH)
+        cols = slice(i * HD, i * HD + HD)
+        keys = jnp.concatenate([kvh[i][b0, 0], kvh[i][b1, 0]], axis=1)
+        scores = jnp.dot(qall[j, at, cols], keys, preferred_element_type=F32)
+        scores = scores * SCALE + bias
+        top = jnp.max(scores, axis=1, keepdims=True)
+        weights = jnp.exp(scores - top).astype(BF)
+        total = jnp.sum(weights.astype(F32), axis=1, keepdims=True)
+        values = jnp.concatenate([kvh[i][b0, 1], kvh[i][b1, 1]], axis=0)
+        got = jnp.dot(weights, values, preferred_element_type=F32)
+        oatt[j, at, cols] = got.astype(BF)
+        stats = jnp.zeros((STRETCH, 128), F32) if i == 0 else ml[j, at, :]
+        ml[j, at, :] = jnp.where(lane == i, top, jnp.where(lane == i + 4, total, stats))
+
+    def attend_slots(a, b, i):
+        def body(n, _):
+            j = jnp.where(n == 0, a, b)
+            for g in range(8):
+                attend(j, g, i)
+            return 0
+
+        lax.fori_loop(0, 1 if a == b else 2, body, 0)
+
+    for j in (1, 2, 3):
         for q in range(4):
             qup[j, q].wait_recv()
             qdown[8 - j, q].wait_recv()
             qsend(j, q)
             qsend(8 - j, q)
-        if j == 1:
-            osend(4)
-            kvsend(10)
-            kvsend(11)
-
-    for n in range(4, 12):
-        kvright[n].wait_recv()
-        kvleft[n].wait_recv()
+            if (j, q) == (1, 1):
+                kvwait(0)
+                attend_slots(0, 0, 0)
+                kvsend(8)
+            if (j, q) == (1, 3):
+                osend(4)
+                kvsend(10)
+            if (j, q) == (2, 0):
+                attend_slots(1, 7, 0)
+            if (j, q) == (2, 2):
+                kvwait(1)
+                attend_slots(0, 0, 1)
+            if (j, q) == (2, 3):
+                attend_slots(1, 7, 1)
+            if (j, q) == (3, 0):
+                attend_slots(2, 6, 0)
+            if (j, q) == (3, 1):
+                kvsend(11)
+                attend_slots(2, 6, 1)
+    attend_slots(3, 5, 0)
+    attend_slots(3, 5, 1)
+    kvwait(2)
+    attend_slots(0, 0, 2)
+    attend_slots(1, 7, 2)
+    attend_slots(2, 6, 2)
+    attend_slots(3, 5, 2)
     oup[4].wait_recv()
     odown[4].wait_recv()
 
     own[2].wait()
     oxs = {}
-    oxs["r"] = send(wog.at[:, x], wog.at[:, x], seq=right)
-    oxs["l"] = send(wog.at[:, x], wog.at[:, x], seq=left)
-
-    lane = lax.broadcasted_iota(jnp.int32, (STRETCH, 128), 1)
-    wide = lax.broadcasted_iota(jnp.int32, (1, 2 * NB_TOK), 1)
-
-    def attend(j, g):
-        r0, r1 = table[ism[j, 0, g]], table[ism[j, 1, g]]
-        off0 = jnp.where(r0 // 32 == z, 0.0, NEG)
-        off1 = jnp.where(r1 // 32 == z, 0.0, NEG)
-        bias = jnp.where(wide < NB_TOK, off0, off1)
-        b0, b1 = r0 % 32, r1 % 32
-        at = pl.ds(pl.multiple_of(g * STRETCH, STRETCH), STRETCH)
-        stats = jnp.zeros((STRETCH, 128), F32)
-        for i in range(W // HD):
-            cols = slice(i * HD, i * HD + HD)
-            keys = jnp.concatenate([kvr[b0, 0, :, cols], kvr[b1, 0, :, cols]], axis=1)
-            scores = jnp.dot(qall[j, at, cols], keys, preferred_element_type=F32)
-            scores = scores * SCALE + bias
-            top = jnp.max(scores, axis=1, keepdims=True)
-            weights = jnp.exp(scores - top).astype(BF)
-            total = jnp.sum(weights.astype(F32), axis=1, keepdims=True)
-            values = jnp.concatenate([kvr[b0, 1, :, cols], kvr[b1, 1, :, cols]], axis=0)
-            got = jnp.dot(weights, values, preferred_element_type=F32)
-            oatt[j, at, cols] = got.astype(BF)
-            stats = jnp.where(lane == i, top, jnp.where(lane == i + 4, total, stats))
-        ml[j, at, :] = stats
-
-    def attend_slots(a, b):
-        def body(i, _):
-            for g in range(4):
-                attend(jnp.where(i < 2, a, b), (i % 2) * 4 + g)
-            return 0
-
-        lax.fori_loop(0, 2 if a == b else 4, body, 0)
-
-    attend_slots(1, 7)
-    for q in range(4):
-        if q < 2:
-            qup[3, q].wait_recv()
-            qsend(3, q)
-        else:
-            qdown[5, q].wait_recv()
-            qsend(5, q)
-    attend_slots(2, 6)
-    for q in range(4):
-        if q < 2:
-            qdown[5, q].wait_recv()
-        else:
-            qup[3, q].wait_recv()
-    attend_slots(3, 5)
+    lower, upper = wog.at[pl.ds(0, 4), x], wog.at[pl.ds(4, 4), x]
+    oxs["r"] = send(lower, lower, seq=right)
+    oxs["l"] = send(upper, upper, seq=left)
+    oxs["r1"] = send(upper, upper, seq=right)
+    oxs["l1"] = send(lower, lower, seq=left)
     for q in range(4):
         (qup if q < 2 else qdown)[4, q].wait_recv()
-    attend_slots(4, 4)
+    for i in range(3):
+        attend_slots(4, 4, i)
+    kvwait(3)
+    attend_slots(4, 4, 3)
 
     sent, sent_stats = {}, {}
 
@@ -469,39 +494,43 @@
             turn_out(k if way == 0 else 8 - k, q)
             rsend(way, k, q, quarter(q))
 
-    for q in (3, 0):
+    first, second = (3, 0), (1, 2)
+    for q in first:
         open_wave(q)
-    for q in (3, 0):
+    attend_slots(3, 5, 3)
+    for q in first:
         hop(3, q)
-    attend_slots(0, 0)
-    for q in (3, 0):
+    for q in second:
+        open_wave(q)
+    attend_slots(2, 6, 3)
+    for q in first:
         hop(2, q)
+    attend_slots(1, 7, 3)
+    attend_slots(0, 0, 3)
+    for q in second:
+        hop(3, q)
     oxs["r"].wait_recv()
     lower = wog.at[pl.ds(0, 4), lo]
     oxs["r2"] = send(lower, lower, seq=right)
     oxs["l"].wait_recv()
     upper = wog.at[pl.ds(4, 4), hi]
     oxs["l2"] = send(upper, upper, seq=left)
-    for q in (3, 0):
+    for q in first:
         hop(1, q)
-    for q in (1, 2):
-        open_wave(q)
-    for q in (3, 0):
+    for q in second:
+        hop(2, q)
+    for q in first:
         join(q)
-    for q in (1, 2):
-        hop(3, q)
-    for name in ("r2", "l2"):
+    for name in ("r1", "l1", "r2", "l2"):
         oxs[name].wait_recv()
-    for q in (3, 0):
+    for q in first:
         for_twin(q)
-    for q in (3, 0):
+    for q in second:
+        hop(1, q)
+    for q in first:
         for_self(q)
-    for q in (1, 2):
-        hop(2, q)
-    for q in (3, 0):
+    for q in first:
         pass_on(q)
-    for q in (1, 2):
-        hop(1, q)
     finish(3)
     edge = give_edge()
     finish(0)
@@ -539,7 +568,7 @@
             vm((NZ, 512, W), BF),
             vm((T + 64, W), F32),
             vm((NZ, T, W), BF),
-            vm((32, 2, NB_TOK, W), BF),
+            *[vm((32, 2, NB_TOK, HD), BF)] * 4,
             vm((NZ, T, W), BF),
             vm((NZ, T, 128), F32),
             vm((2, 4, T, W), BF),
@@ -561,7 +590,7 @@
             vm((64, W), BF),
             vm((64, W), BF),
             vm((4, QT, 512), BF),
-            pltpu.SemaphoreType.DMA((8,)),
+            pltpu.SemaphoreType.DMA((12,)),
             pltpu.SemaphoreType.DMA((4,)),
             pltpu.SemaphoreType.DMA((N_COPIES,)),
             pltpu.SemaphoreType.DMA((N_COPIES,)),

time: 178 us -> 173 us (0.972)
  Pallas kernels: 174 us -> 168 us
    pallas_call x1, Pallas kernels: 174 us -> 168 us  [exchange(): pl.pallas_call(kernel, out_shape=jax.ShapeDtypeStruct((T, W), BF), in_spe...]
where the time goes in v4:
time: 173 us; the launch traced here: 170 us
  Pallas kernels  168 us (97%)
  local copies, waits for them, and re-layouts  1.87 us (1%)
    pallas_call x1, Pallas kernels, exchange(): pl.pallas_call(kernel, out_shape=jax.ShapeDtypeStruct((T, W), BF), in_spe...  168 us

profile of v4, /device:TPU:1, one launch (start us, length us, event | category | flops | bytes accessed | tf_op | source)
XLA Modules:
  0.0 170.4 jit_solution(4436056109240360088)
XLA Ops:
  0.0 168.5 %shard_map.64 = bf16[512,512]{1,0:T(8,128)(2,1)} custom-call(bf16[512,4096]{1,0:T(8,128)(2,1)} %states.1, bf16[128,512]{1,0:T(8,128)(2,1)} %wq.1, bf16[512,128]{1,0:T(8,128)(2,1)} %wo.1, bf16[8,2,128,512]{3,2,1,0:T(8,128)(2,1)} %kv.1, s32[2,8]{1,0:T(2,128)} %bitcast.1, s32[256]{0:T(256)} %table.1), custom_call_target="tpu_custom_call" | custom-call | flops 8000000000 | bytes 8388608 | tf_op jit(solution)/shard_map/pallas_call | solution.py:561
  168.5 1.9 %copy.8 = bf16[512,512]{1,0:T(8,128)(2,1)} copy(bf16[512,512]{1,0:T(8,128)(2,1)} %shard_map.64) | data formatting | bytes 1048576

commit v5 on v4

--- a/solution.py
+++ b/solution.py
@@ -137,14 +137,13 @@
     wx[2] = send(wqg.at[0, arows(1, 0, AU)], wqg.at[0, arows(1, 0, AU)], seq=right)
     wx[3].wait_recv()
     wx[4] = send(wqg.at[0, arows(3, AU, PA - AU)], wqg.at[0, arows(3, AU, PA - AU)], seq=left)
-    bsend(2)
     wsend(0, 1)
     wsend(0, 3)
+    bsend(2)
     iids = [send(ids, iall.at[i], seq=(s + NX * i) % NSEQ) for i in range(1, NZ)]
     hcols = pl.ds(pl.multiple_of(h * W, W), W)
     tail = st.at[pl.ds(T, 64), hcols]
     first_rows = send(states.at[pl.ds(0, 64), hcols], tail, seq=before)
-    bsend(3)
 
     lo, hi = (x + 3) % NX, (x + 1) % NX
     kvright, kvleft = {}, {}
@@ -170,12 +169,22 @@
             kvright[n].wait_recv()
             kvleft[n].wait_recv()
 
+    def forward(j, d):
+        wup[j, d].wait_recv()
+        wdown[8 - j, d].wait_recv()
+        wsend(j, d)
+        wsend(8 - j, d)
+
     kvsend(0)
     wx[2].wait_recv()
     wx[4].wait_recv()
     wsend(0, 2)
+    bsend(3)
+    forward(1, 0)
+    forward(1, 1)
+    kvsend(1)
     bsend(4)
-    kvsend(1)
+    forward(1, 3)
     first_rows.wait_recv()
     others = [send(tail, tail, head=(h + i) % NHEAD) for i in range(1, NHEAD)]
     own[1].wait()
@@ -185,6 +194,7 @@
     bx["r"] = send(wqg.at[:, brows(x)], wqg.at[:, brows(x)], seq=right)
     bx["l"] = send(wqg.at[:, brows(x)], wqg.at[:, brows(x)], seq=left)
     kvsend(2)
+    forward(1, 2)
 
     oup, odown = {}, {}
 
@@ -219,45 +229,43 @@
 
         lax.fori_loop(0, 3, body, 0)
 
-    order = (0, 1, 3, 2)
-    for j in (1, 2, 3):
-        for d in order:
-            wup[j, d].wait_recv()
-            wdown[8 - j, d].wait_recv()
-            wsend(j, d)
-            wsend(8 - j, d)
-        if j == 1:
-            osend(1)
-            bx["r"].wait_recv()
-            at = (pl.ds(0, 4), brows(lo))
-            bx["r2"] = send(wqg.at[at], wqg.at[at], seq=right)
-            bx["l"].wait_recv()
-            at = (pl.ds(4, 4), brows(hi))
-            bx["l2"] = send(wqg.at[at], wqg.at[at], seq=left)
-            kvsend(3)
-        if j == 2:
-            osend(2)
-            kvsend(4)
-            kvsend(6)
-            own[0].wait()
-            for copy in others:
-                copy.wait_recv()
-            for copy in others:
-                copy.wait_send()
-                del started[id(copy)]
-
-            @pl.when(s == NSEQ - 1)
-            def _():
-                st[pl.ds(T, 64), :] = jnp.zeros((64, NHEAD * W), BF)
-
-        if j == 3:
-            osend(3)
-            kvsend(5)
-            kvsend(7)
-            bx["r2"].wait_recv()
-            bx["l2"].wait_recv()
-            for n in (0, 1, 7, 2, 6, 3, 5):
-                multiply(n)
+    osend(1)
+    forward(2, 0)
+    forward(2, 1)
+    bx["r"].wait_recv()
+    at = (pl.ds(0, 4), brows(lo))
+    bx["r2"] = send(wqg.at[at], wqg.at[at], seq=right)
+    bx["l"].wait_recv()
+    at = (pl.ds(4, 4), brows(hi))
+    bx["l2"] = send(wqg.at[at], wqg.at[at], seq=left)
+    kvsend(3)
+    forward(2, 3)
+    forward(2, 2)
+    osend(2)
+    kvsend(4)
+    kvsend(6)
+    forward(3, 0)
+    own[0].wait()
+    for copy in others:
+        copy.wait_recv()
+    for copy in others:
+        copy.wait_send()
+        del started[id(copy)]
+    forward(3, 1)
+
+    @pl.when(s == NSEQ - 1)
+    def _():
+        st[pl.ds(T, 64), :] = jnp.zeros((64, NHEAD * W), BF)
+
+    forward(3, 3)
+    forward(3, 2)
+    osend(3)
+    kvsend(5)
+    kvsend(7)
+    bx["r2"].wait_recv()
+    bx["l2"].wait_recv()
+    for n in (0, 1, 7, 2, 6, 3, 5):
+        multiply(n)
     for d in (0, 1):
         wup[4, d].wait_recv()
     for d in (2, 3):
@@ -531,19 +539,19 @@
         for_self(q)
     for q in first:
         pass_on(q)
-    finish(3)
-    edge = give_edge()
-    finish(0)
     join(1)
     for_twin(1)
     join(2)
     for_twin(2)
     for_self(1)
     for_self(2)
+    finish(3)
+    edge = give_edge()
+    finish(0)
+    pass_on(1)
+    pass_on(2)
     take_edge(edge)
     write(0)
-    pass_on(1)
-    pass_on(2)
     finish(1)
     write(1)
     finish(2)

time: 173 us -> 164 us (0.948)
  Pallas kernels: 168 us -> 161 us
    pallas_call x1, Pallas kernels: 168 us -> 161 us  [exchange(): pl.pallas_call(kernel, out_shape=jax.ShapeDtypeStruct((T, W), BF), in_spe...]
where the time goes in v5:
time: 164 us; the launch traced here: 163 us
  Pallas kernels  161 us (98%)
  local copies, waits for them, and re-layouts  1.87 us (1%)
    pallas_call x1, Pallas kernels, exchange(): pl.pallas_call(kernel, out_shape=jax.ShapeDtypeStruct((T, W), BF), in_spe...  161 us

profile of v5, /device:TPU:1, one launch (start us, length us, event | category | flops | bytes accessed | tf_op | source)
XLA Modules:
  0.0 162.6 jit_solution(10895640400791244308)
XLA Ops:
  0.0 160.7 %shard_map.64 = bf16[512,512]{1,0:T(8,128)(2,1)} custom-call(bf16[512,4096]{1,0:T(8,128)(2,1)} %states.1, bf16[128,512]{1,0:T(8,128)(2,1)} %wq.1, bf16[512,128]{1,0:T(8,128)(2,1)} %wo.1, bf16[8,2,128,512]{3,2,1,0:T(8,128)(2,1)} %kv.1, s32[2,8]{1,0:T(2,128)} %bitcast.1, s32[256]{0:T(256)} %table.1), custom_call_target="tpu_custom_call" | custom-call | flops 8000000000 | bytes 8388608 | tf_op jit(solution)/shard_map/pallas_call | solution.py:569
  160.7 1.9 %copy.8 = bf16[512,512]{1,0:T(8,128)(2,1)} copy(bf16[512,512]{1,0:T(8,128)(2,1)} %shard_map.64) | data formatting | bytes 1048576

commit v6 on v5

--- a/solution.py
+++ b/solution.py
@@ -34,7 +34,7 @@
 def kernel(
     states, wq, wo, kv, ids, table, out,
     st, wqg, acc, qall, kv0, kv1, kv2, kv3, oatt, ml, ro, sw, rw, wog, iall, ism,
-    ctx, ps, pr, tf, t2s, t2r, t1s, t1r, kraw, fin, edge_s, edge_r, ost, lsem, osem, ssem, rsem,
+    ctx, ps, pr, tf, t2s, t2r, t1s, t1r, kraw, fin, edge_s, edge_r, lsem, ssem, rsem,
 ):
     s, h = lax.axis_index("seq"), lax.axis_index("head")
     z, x, y, c = s // NX, s % NX, h // 2, h % 2
@@ -284,7 +284,8 @@
 
     for q in range(4):
         qall[0, quarter(q), :] = acc[pl.ds(63 + q * QT, QT), :].astype(BF)
-        qsend(0, q)
+        if q < 2:
+            qsend(0, q)
 
     kvsend(9)
     for copy in iids:
@@ -293,6 +294,11 @@
     scalars = pltpu.make_async_copy(iall, ism, lsem.at[5])
     scalars.start()
     scalars.wait()
+    for q in (2, 3):
+        for copy in (qup[1, q - 2], qdown[7, q - 2]):
+            copy.wait_send()
+            del started[id(copy)]
+        qsend(0, q)
 
     lane = lax.broadcasted_iota(jnp.int32, (STRETCH, 128), 1)
     wide = lax.broadcasted_iota(jnp.int32, (1, 2 * NB_TOK), 1)
@@ -428,7 +434,7 @@
             mixed = mixed + fe[:, i : i + 1] * oatt[0, at, cols].astype(F32)
             ctx[q, :, cols] = mixed.astype(BF)
 
-    pairs, seconds, thirds, written = {}, {}, {}, []
+    pairs, seconds, thirds = {}, {}, {}
 
     far_first = (2, 1, 3, 0)
 
@@ -481,10 +487,7 @@
         fin[pl.ds(0, 64), :] = jnp.where(s == 0, 0.0, edge_r[...].astype(F32))
 
     def write(i):
-        ost[i] = fin[pl.ds(i * QT + 1, QT), :].astype(BF)
-        copy = pltpu.make_async_copy(ost.at[i], out.at[quarter(i)], osem.at[i])
-        copy.start()
-        written.append(copy)
+        out[quarter(i), :] = fin[pl.ds(i * QT + 1, QT), :].astype(BF)
 
     def open_wave(q):
         turn_out(4, q)
@@ -557,8 +560,6 @@
     finish(2)
     write(2)
     write(3)
-    for copy in written:
-        copy.wait()
     for copy in started.values():
         copy.wait_send()
 
@@ -570,7 +571,7 @@
         kernel,
         out_shape=jax.ShapeDtypeStruct((T, W), BF),
         in_specs=[anywhere] * 5 + [pl.BlockSpec(memory_space=pltpu.SMEM)],
-        out_specs=anywhere,
+        out_specs=pl.BlockSpec(memory_space=vm),
         scratch_shapes=[
             vm((T + 64, NHEAD * W), BF),
             vm((NZ, 512, W), BF),
@@ -597,9 +598,7 @@
             vm((T + 64, W), F32),
             vm((64, W), BF),
             vm((64, W), BF),
-            vm((4, QT, 512), BF),
             pltpu.SemaphoreType.DMA((12,)),
-            pltpu.SemaphoreType.DMA((4,)),
             pltpu.SemaphoreType.DMA((N_COPIES,)),
             pltpu.SemaphoreType.DMA((N_COPIES,)),
         ],

time: 164 us -> 164 us (level)
  no operation moved by 1% of the time
where the time goes in v6:
time: 164 us; the launch traced here: 163 us
  Pallas kernels  161 us (98%)
  local copies, waits for them, and re-layouts  1.87 us (1%)
    pallas_call x1, Pallas kernels, exchange(): pl.pallas_call(kernel, out_shape=jax.ShapeDtypeStruct((T, W), BF), in_spe...  161 us

profile of v6, /device:TPU:1, one launch (start us, length us, event | category | flops | bytes accessed | tf_op | source)
XLA Modules:
  0.0 162.7 jit_solution(5564867073572940019)
XLA Ops:
  0.0 160.8 %shard_map.64 = bf16[512,512]{1,0:T(8,128)(2,1)} custom-call(bf16[512,4096]{1,0:T(8,128)(2,1)} %states.1, bf16[128,512]{1,0:T(8,128)(2,1)} %wq.1, bf16[512,128]{1,0:T(8,128)(2,1)} %wo.1, bf16[8,2,128,512]{3,2,1,0:T(8,128)(2,1)} %kv.1, s32[2,8]{1,0:T(2,128)} %bitcast.1, s32[256]{0:T(256)} %table.1), custom_call_target="tpu_custom_call" | custom-call | flops 8000000000 | bytes 8388608 | tf_op jit(solution)/shard_map/pallas_call | solution.py:570
  160.8 1.9 %copy.8 = bf16[512,512]{1,0:T(8,128)(2,1)} copy(bf16[512,512]{1,0:T(8,128)(2,1)} %shard_map.64) | data formatting | bytes 1048576
